TPU v7x, 128 devices: a whole 4x4x4 slice. The times are simulated.
128 devices in a mesh: row: 16 (over x, z), col: 8 (over y, core).
Axes of the slice: x: 4, y: 4, z: 4, core: 2. Of those that a mesh axis runs over, the one named last changes fastest.
Arguments:
- parent_front: float32 [128, 128, 128, 128], P('row', 'col'), as said below
- child_updates: float32 [128, 64, 128, 128], P('row', 'col'), as said below
- child_mask: int32 [128, 64], P('row', 'col'), may hold values from 0 to 1, as said below
- child_map: int32 [2, 64], replicated, may hold values from 0 to 127, as said below
Outputs:
- factored: float32 [128, 128, 128, 128], P('row', 'col')
Inputs may be any that keep to these rules, and one draw needn't show every extreme that they name: `parent_front`: symmetric as a matrix of order 16384; with any admissible child updates the assembled front is positive definite. `child_updates`: each child's update is symmetric as a matrix of order 64 * 128. `child_mask`: symmetric for each child: block (a, b) is nonzero exactly when block (b, a) is. `child_map`: the 64 entries of one child are distinct. For each child and each t < 8, among the child blocks t + 8 i at most 1 share a residue modulo 2 * 8 and at most 1 share a residue modulo 8; both bounds are reached in every draw.
All inputs are finite; a program needn't handle non-finite values.
Results may differ from a plain program's by a relative error of at most 0.00005.
Values sent between devices are 32-bit elements; how exact they have to be, the bound alone decides.
No kernel may reach another device: no remote copies, remote signals or barrier semaphores. Data moves between devices by JAX's collectives and lax.ppermute only.
A program may use at most 128 MiB of HBM per device.

v0:
```python
import jax
import jax.numpy as jnp
from jax import lax
from jax.sharding import PartitionSpec as P

PW = 4
PANELS = 2


exact_precision = lax.Precision.HIGHEST


def from_root(value, axis, source):
    kept = jnp.where(lax.axis_index(axis) == source, value, 0).astype(value.dtype)
    return lax.psum(kept, axis)


def rank_among(keys):
    count = keys.shape[-1]
    places = jnp.arange(count)
    same_key = keys[..., :, None] == keys[..., None, :]
    earlier = places[None, :] < places[:, None]
    return jnp.sum(jnp.logical_and(same_key, earlier), axis=-1)


def shards(parent_front, child_updates, child_mask, child_map):
    row_count = lax.axis_size("row")
    col_count = lax.axis_size("col")
    row_index = lax.axis_index("row")
    col_index = lax.axis_index("col")
    local_rows = parent_front.shape[0]
    local_cols = parent_front.shape[1]
    edge_size = parent_front.shape[2]
    child_blocks = child_updates.shape[0]
    row_groups = row_count // col_count
    row_slots = -(-child_blocks // row_count)
    col_slots = -(-child_blocks // col_count)
    slot_total = row_slots * col_slots
    positions = jnp.arange(child_blocks)
    own_map = jnp.take(child_map, row_index // col_count, axis=0)
    row_parent = jnp.take(own_map, positions * col_count + row_index % col_count)
    col_parent = jnp.take(own_map, positions * col_count + col_index)
    dest_row = row_parent % row_count
    dest_col = col_parent % col_count
    slot_place = rank_among(dest_row)[:, None] * col_slots + rank_among(dest_col)[None, :]
    live_blocks = child_updates * child_mask.astype(jnp.float32)[:, :, None, None]
    outgoing = jnp.zeros((row_count, col_count, slot_total, edge_size, edge_size), jnp.float32)
    outgoing = outgoing.at[dest_row[:, None], dest_col[None, :], slot_place].add(live_blocks)
    merged = outgoing.reshape(row_count * col_count, slot_total, edge_size, edge_size)
    arrived = lax.all_to_all(merged, ("row", "col"), split_axis=0, concat_axis=0, tiled=True)
    sender_rows = jnp.arange(row_count)
    sender_side = sender_rows // col_count
    row_keys = child_map[
        sender_side[:, None], positions[None, :] * col_count + (sender_rows % col_count)[:, None]
    ]
    row_hit = row_keys % row_count == row_index
    row_pick = jnp.logical_and(
        row_hit[:, :, None],
        rank_among(row_keys % row_count)[:, :, None] == jnp.arange(row_slots)[None, None, :],
    )
    row_target = jnp.sum(row_pick * (row_keys // row_count)[:, :, None], axis=1)
    row_valid = jnp.any(row_pick, axis=1)
    col_keys = child_map[:, positions[None, :] * col_count + jnp.arange(col_count)[:, None]]
    col_hit = col_keys % col_count == col_index
    col_pick = jnp.logical_and(
        col_hit[..., None], rank_among(col_keys % col_count)[..., None] == jnp.arange(col_slots)
    )
    col_target = jnp.sum(col_pick * (col_keys // col_count)[..., None], axis=2)
    col_valid = jnp.any(col_pick, axis=2)
    target = row_target[:, None, :, None] * local_cols + col_target[sender_side][:, :, None, :]
    valid = jnp.logical_and(row_valid[:, None, :, None], col_valid[sender_side][:, :, None, :])
    target = jnp.where(valid, target, local_rows * local_cols).reshape(-1)
    gains = jnp.zeros((local_rows * local_cols, edge_size, edge_size), jnp.float32)
    gains = gains.at[target].add(arrived.reshape(-1, edge_size, edge_size), mode="drop")
    front = parent_front + gains.reshape(local_rows, local_cols, edge_size, edge_size)
    my_rows = jnp.arange(local_rows) * row_count + row_index
    my_cols = jnp.arange(local_cols) * col_count + col_index
    panel_width = PW * edge_size
    factored_blocks = PANELS * PW
    for panel_index in range(PANELS):
        first = panel_index * PW
        after = first + PW
        low_col = first // col_count
        high_col = (after - 1) // col_count
        col_span = high_col - low_col + 1
        gathered = lax.all_gather(front[:, low_col : high_col + 1], "col", axis=1, tiled=True)
        col_order = [
            g % col_count * col_span + g // col_count - low_col for g in range(first, after)
        ]
        panel_rows = jnp.take(gathered, jnp.array(col_order, dtype=jnp.int32), axis=1)
        low_row = first // row_count
        high_row = (after - 1) // row_count
        row_span = high_row - low_row + 1
        stacked = lax.all_gather(panel_rows[low_row : high_row + 1], "row", axis=0, tiled=True)
        row_order = [
            g % row_count * row_span + g // row_count - low_row for g in range(first, after)
        ]
        diag_blocks = jnp.take(stacked, jnp.array(row_order, dtype=jnp.int32), axis=0)
        diag_matrix = diag_blocks.transpose(0, 2, 1, 3).reshape(panel_width, panel_width)
        factor = jnp.linalg.cholesky(diag_matrix)
        inverse = lax.linalg.triangular_solve(
            factor, jnp.eye(panel_width, dtype=jnp.float32), left_side=True, lower=True
        )
        rows_matrix = panel_rows.transpose(0, 2, 1, 3).reshape(local_rows * edge_size, panel_width)
        solved = jnp.dot(rows_matrix, inverse.T, precision=exact_precision).reshape(
            local_rows, edge_size, panel_width
        )
        factor_rows = factor.reshape(PW, edge_size, panel_width)
        inside_panel = jnp.logical_and(my_rows >= first, my_rows < after)
        position = jnp.clip(my_rows - first, 0, PW - 1)
        from_factor = jnp.where(inside_panel[:, None, None], factor_rows[position], 0.0)
        lower_rows = jnp.where((my_rows >= after)[:, None, None], solved, from_factor)
        lower_blocks = lower_rows.reshape(local_rows, edge_size, PW, edge_size).transpose(
            0, 2, 1, 3
        )
        col_pick_table = (my_cols[:, None] - first == jnp.arange(PW)[None, :]).astype(jnp.float32)
        placed = jnp.einsum(
            "mp,lpxy->lmxy", col_pick_table, lower_blocks, precision=exact_precision
        )
        panel_cols = jnp.logical_and(my_cols >= first, my_cols < after)
        front = jnp.where(panel_cols[None, :, None, None], placed, front)
        received = []
        for group in range(row_groups):
            received.append(from_root(lower_rows, "row", col_index + col_count * group))
        column_lower = jnp.stack(received, axis=1).reshape(local_cols, edge_size, panel_width)
        update = jnp.einsum("lxw,myw->lmxy", lower_rows, column_lower, precision=exact_precision)
        trailing = jnp.logical_and((my_rows >= after)[:, None], (my_cols >= after)[None, :])
        kept_rows = jnp.logical_or(
            (my_cols < factored_blocks)[None, :], (my_rows >= factored_blocks)[:, None]
        )
        trailing = jnp.logical_and(trailing, kept_rows)
        front = front - jnp.where(trailing[:, :, None, None], update, 0.0)
    return front


def solution(mesh):
    in_specs = (P("row", "col", None, None), P("row", "col", None, None), P("row", "col"), P())
    out_specs = P("row", "col", None, None)
    return jax.shard_map(shards, mesh=mesh, in_specs=in_specs, out_specs=out_specs, check_vma=False)
```

profile of v0, /device:TPU:1, one launch (start us, length us, event | category | flops | bytes accessed | tf_op | source)
XLA Modules:
  0.0 1027.9 jit_solution(4119021330335804920)
XLA Ops:
  18.7 13.9 %scatter_fusion = f32[16,8,128,128]{3,2,1,0:T(8,128)} fusion(f32[16,8,128,128]{3,2,1,0:T(8,128)} %broadcast.1149, s32[64]{0:T(128)S(1)} %reshape.863, f32[64,128,128]{2,1,0:T(8,128)} %bitcast.251), kind=kCustom, calls=%fused_computation.12 | custom fusion | flops 1048576 | bytes 12583424 | tf_op jit(solution)/shard_map/scatter-add | solution.py:48
  32.6 12.0 %all-to-all-start = ((f32[128,1,128,128]{3,2,1,0:T(8,128)}), f32[128,1,128,128]{3,2,1,0:T(8,128)}, u32[]{:S(2)}, u32[]{:S(2)}) async-start(f32[128,1,128,128]{3,2,1,0:T(8,128)} %bitcast.248), calls=%async_computation | async-start | bytes 16777216 | tf_op jit(solution)/shard_map/all_to_all | solution.py:50
  49.7 101.3 %all-to-all-done = f32[128,1,128,128]{3,2,1,0:T(8,128)} async-done(((f32[128,1,128,128]{3,2,1,0:T(8,128)}), f32[128,1,128,128]{3,2,1,0:T(8,128)}, u32[]{:S(2)}, u32[]{:S(2)}) %all-to-all-start) | async-done | bytes 8388640 | tf_op jit(solution)/shard_map/all_to_all | solution.py:50
  155.5 25.6 %scatter_fusion.1 = f32[128,128,128]{2,1,0:T(8,128)} fusion(f32[128,128,128]{2,1,0:T(8,128)} %broadcast_in_dim.123, s32[128]{0:T(128)S(1)} %fusion.108, f32[128,128,128]{2,1,0:T(8,128)} %bitcast.7), kind=kCustom, calls=%fused_computation.13 | custom fusion | flops 2097152 | bytes 25166336 | tf_op jit(solution)/shard_map/scatter-add | solution.py:74
  181.1 22.4 %copy_add_fusion = f32[8,16,128,128]{3,1,2,0:T(8,128)} fusion(f32[8,16,128,128]{3,2,1,0:T(8,128)} %bitcast.247, f32[8,16,128,128]{3,2,1,0:T(8,128)} %param.17), kind=kLoop, calls=%fused_computation.24 | loop fusion | flops 2097152 | bytes 25165824 | tf_op jit(solution)/shard_map/add | solution.py:75
  206.9 32.3 %all-gather.5.cloned.1.call-done = f32[8,8,128,128]{3,2,0,1:T(8,128)} async-done(((f32[8,1,128,128]{3,2,0,1:T(8,128)}), f32[8,8,128,128]{3,2,0,1:T(8,128)}) %all-gather.5.cloned.1.call-update) | async-done | bytes 4194320 | tf_op jit(solution)/shard_map/all_gather | solution.py:86
  253.1 49.3 %all-gather.7.cloned.1.call-done = f32[16,4,128,128]{3,2,0,1:T(8,128)} async-done(((f32[1,4,128,128]{3,2,0,1:T(8,128)}), f32[16,4,128,128]{3,2,0,1:T(8,128)}) %all-gather.7.cloned.1.call-update) | async-done | bytes 4194320 | tf_op jit(solution)/shard_map/all_gather | solution.py:94
  309.5 11.7 %cholesky.286 = f32[128,128]{1,0:T(8,128)S(1)} custom-call(f32[128,128]{1,0:T(8,128)S(1)} %cholesky.426), custom_call_target="Cholesky" | custom-call | tf_op jit(solution)/shard_map/jit(cholesky)/cholesky | solution.py:100
  321.4 9.8 custom-call.31
  333.8 11.7 %cholesky.305 = f32[128,128]{1,0:T(8,128)S(1)} custom-call(f32[128,128]{1,0:T(8,128)S(1)} %cholesky.430), custom_call_target="Cholesky" | custom-call | tf_op jit(solution)/shard_map/jit(cholesky)/cholesky | solution.py:100
  346.9 9.9 custom-call.32
  358.4 11.7 %cholesky.326 = f32[128,128]{1,0:T(8,128)S(1)} custom-call(f32[128,128]{1,0:T(8,128)S(1)} %cholesky.435), custom_call_target="Cholesky" | custom-call | tf_op jit(solution)/shard_map/jit(cholesky)/cholesky | solution.py:100
  370.9 9.8 custom-call.33
  382.1 12.1 %cholesky.343 = f32[128,128]{1,0:T(8,128)S(1)} custom-call(f32[128,128]{1,0:T(8,128)S(1)} %convolution_subtract_fusion.11), custom_call_target="Cholesky" | custom-call | tf_op jit(solution)/shard_map/jit(cholesky)/cholesky | solution.py:100
  398.8 12.0 %while.5 = (s32[]{:T(128)}, f32[512,512]{1,0:T(8,128)}, s32[4,2]{0,1:T(2,128)S(1)}, f32[4,128,128]{2,1,0:T(8,128)S(1)}, s32[]{:T(128)}) while((s32[]{:T(128)}, f32[512,512]{1,0:T(8,128)}, s32[4,2]{0,1:T(2,128)S(1)}, f32[4,128,128]{2,1,0:T(8,128)S(1)}, s32[]{:T(128)}) %tuple.78), condition=%wide.while_cond, body=%wide.while_body.sunk | while | flops 2 | bytes 131181 | solution.py:101
  410.8 39.3 %custom-call.34 = f32[4,128,128]{1,2,0:T(8,128)S(1)} custom-call(f32[4,128,128]{2,1,0:T(8,128)S(1)} %get-tuple-element.35), custom_call_target="InvertDiagBlocksLowerTriangular" | custom-call | tf_op jit(solution)/shard_map/triangular_solve/custom-call.3 | solution.py:101
  458.9 9.5 select_select_fusion.1
  473.2 101.3 %all-reduce.8.cloned.1.call-done = (f32[8,1,128,512]{3,2,0,1:T(8,128)}, f32[8,1,128,512]{3,2,0,1:T(8,128)}) async-done(((f32[8,1,128,512]{3,2,0,1:T(8,128)}, f32[8,1,128,512]{3,2,0,1:T(8,128)}), (f32[8,1,128,512]{3,2,0,1:T(8,128)}, f32[8,1,128,512]{3,2,0,1:T(8,128)})) %all-reduce.8.cloned.1.call-update) | async-done | bytes 4194320 | tf_op jit(solution)/shard_map/psum | solution.py:15
  577.9 15.9 %fusion.5 = f32[16,128,8,128]{3,1,2,0:T(8,128)} fusion(f32[16,128,512,1]{2,1,3,0:T(8,128)S(1)} %bitcast.249, f32[8,128,512]{2,1,0:T(8,128)S(1)} %select_select_fusion.1), kind=kOutput, calls=%fused_computation.30 | convolution fusion | flops 12884901888 | bytes 14680064 | tf_op jit(solution)/shard_map/lxw,myw->lmxy/dot_general | solution.py:126
  615.6 32.4 %all-gather.9.cloned.1.call-done = f32[8,8,128,128]{3,2,0,1:T(8,128)} async-done(((f32[8,1,128,128]{3,2,0,1:T(8,128)}), f32[8,8,128,128]{3,2,0,1:T(8,128)}) %all-gather.9.cloned.1.call-update) | async-done | bytes 4194320 | tf_op jit(solution)/shard_map/all_gather | solution.py:86
  658.6 49.1 %all-gather.11.cloned.1.call-done = f32[16,4,128,128]{3,2,0,1:T(8,128)} async-done(((f32[1,4,128,128]{3,2,0,1:T(8,128)}), f32[16,4,128,128]{3,2,0,1:T(8,128)}) %all-gather.11.cloned.1.call-update) | async-done | bytes 4194320 | tf_op jit(solution)/shard_map/all_gather | solution.py:94
  714.7 11.7 %cholesky.358 = f32[128,128]{1,0:T(8,128)S(1)} custom-call(f32[128,128]{1,0:T(8,128)S(1)} %cholesky.439), custom_call_target="Cholesky" | custom-call | tf_op jit(solution)/shard_map/jit(cholesky)/cholesky | solution.py:100
  726.6 9.8 custom-call.35
  738.9 11.7 %cholesky.377 = f32[128,128]{1,0:T(8,128)S(1)} custom-call(f32[128,128]{1,0:T(8,128)S(1)} %cholesky.443), custom_call_target="Cholesky" | custom-call | tf_op jit(solution)/shard_map/jit(cholesky)/cholesky | solution.py:100
  751.9 10.0 custom-call.36
  763.5 11.7 %cholesky.398 = f32[128,128]{1,0:T(8,128)S(1)} custom-call(f32[128,128]{1,0:T(8,128)S(1)} %cholesky.448), custom_call_target="Cholesky" | custom-call | tf_op jit(solution)/shard_map/jit(cholesky)/cholesky | solution.py:100
  775.9 9.8 custom-call.37
  787.1 11.9 %cholesky.415 = f32[128,128]{1,0:T(8,128)S(1)} custom-call(f32[128,128]{1,0:T(8,128)S(1)} %convolution_subtract_fusion.10), custom_call_target="Cholesky" | custom-call | tf_op jit(solution)/shard_map/jit(cholesky)/cholesky | solution.py:100
  803.3 11.2 %while.6 = (s32[]{:T(128)}, f32[512,512]{1,0:T(8,128)}, s32[4,2]{0,1:T(2,128)S(1)}, f32[4,128,128]{2,1,0:T(8,128)S(1)}, s32[]{:T(128)}) while((s32[]{:T(128)}, f32[512,512]{1,0:T(8,128)}, s32[4,2]{0,1:T(2,128)S(1)}, f32[4,128,128]{2,1,0:T(8,128)S(1)}, s32[]{:T(128)}) %tuple.98), condition=%wide.while_cond.clone, body=%wide.while_body.clone.sunk | while | flops 2 | bytes 131181 | solution.py:101
  814.5 39.3 %custom-call.38 = f32[4,128,128]{1,2,0:T(8,128)S(1)} custom-call(f32[4,128,128]{2,1,0:T(8,128)S(1)} %get-tuple-element.36), custom_call_target="InvertDiagBlocksLowerTriangular" | custom-call | tf_op jit(solution)/shard_map/triangular_solve/custom-call.3 | solution.py:101
  875.8 101.6 %all-reduce.6.cloned.1.call-done = (f32[8,1,128,512]{3,2,0,1:T(8,128)}, f32[8,1,128,512]{3,2,0,1:T(8,128)}) async-done(((f32[8,1,128,512]{3,2,0,1:T(8,128)}, f32[8,1,128,512]{3,2,0,1:T(8,128)}), (f32[8,1,128,512]{3,2,0,1:T(8,128)}, f32[8,1,128,512]{3,2,0,1:T(8,128)})) %all-reduce.6.cloned.1.call-update) | async-done | bytes 4194320 | tf_op jit(solution)/shard_map/psum | solution.py:15
  980.8 16.3 %fusion.2 = f32[16,128,8,128]{3,1,2,0:T(8,128)} fusion(f32[16,128,512,1]{2,1,3,0:T(8,128)S(1)} %bitcast.250, f32[8,128,512]{2,1,0:T(8,128)S(1)} %select_select_fusion), kind=kOutput, calls=%fused_computation.27 | convolution fusion | flops 12884901888 | bytes 14680064 | tf_op jit(solution)/shard_map/lxw,myw->lmxy/dot_general | solution.py:126
  (214 shorter events, 193.5 us)
Async XLA Ops:
  32.6 12.0 %copy-start = (s32[2,64]{1,0:T(2,128)S(1)}, s32[2,64]{1,0:T(2,128)}, u32[]{:S(2)}) copy-start(s32[2,64]{1,0:T(2,128)} %param.20) | copy-start | bytes 1540
  32.6 118.4 %all-to-all-start = ((f32[128,1,128,128]{3,2,1,0:T(8,128)}), f32[128,1,128,128]{3,2,1,0:T(8,128)}, u32[]{:S(2)}, u32[]{:S(2)}) async-start(f32[128,1,128,128]{3,2,1,0:T(8,128)} %bitcast.248), calls=%async_computation | async-start | bytes 16777216 | tf_op jit(solution)/shard_map/all_to_all | solution.py:50
  44.6 194.6 %all-gather.5.cloned.1.call-start = ((), (), s32[]{:S(2)}) async-start(), calls=%async_computation.1 | async-start | bytes 4718592 | tf_op jit(solution)/shard_map/all_gather | solution.py:86
  206.8 95.5 %all-gather.7.cloned.1.call-start = ((), (), s32[]{:S(2)}) async-start(), calls=%async_computation.2 | async-start | bytes 4456448 | tf_op jit(solution)/shard_map/all_gather | solution.py:94
  251.0 323.5 %all-reduce.8.cloned.1.call-start = ((), (), s32[]{:S(2)}) async-start(), calls=%async_computation.6 | async-start | bytes 8388608 | tf_op jit(solution)/shard_map/psum | solution.py:15
  308.6 1.0 copy-start.6
  452.2 6.7 copy-start.5
  454.1 4.8 copy-start.9
  471.1 176.9 %all-gather.9.cloned.1.call-start = ((), (), s32[]{:S(2)}) async-start(), calls=%async_computation.3 | async-start | bytes 4718592 | tf_op jit(solution)/shard_map/all_gather | solution.py:86
  593.7 9.3 copy-start.3
  603.1 12.5 %copy-start.10 = (s32[4]{0:T(128)S(1)}, s32[4]{0:T(128)}, u32[]{:S(2)}) copy-start(s32[4]{0:T(128)} %constant.415) | copy-start | bytes 52
  611.2 3.2 copy-start.1
  615.5 92.2 %all-gather.11.cloned.1.call-start = ((), (), s32[]{:S(2)}) async-start(), calls=%async_computation.4 | async-start | bytes 4456448 | tf_op jit(solution)/shard_map/all_gather | solution.py:94
  656.3 321.1 %all-reduce.6.cloned.1.call-start = ((), (), s32[]{:S(2)}) async-start(), calls=%async_computation.5 | async-start | bytes 8388608 | tf_op jit(solution)/shard_map/psum | solution.py:15
  713.7 1.0 copy-start.7
  855.9 6.0 copy-start.4
  857.8 4.1 copy-start.8
  997.1 9.3 copy-start.2
Sparse Core Ops, SparseCore 0:
  206.9 32.2 all-gather.4
  251.1 51.2 all-gather.6
  471.2 103.2 all-reduce.7
  615.6 32.3 all-gather.8
  656.4 51.2 all-gather.10
  874.1 103.1 all-reduce.5
where the time goes:
time: 1030 us
  waiting for transfers between devices  467 us (45%)
  other arithmetic  323 us (31%)
  local copies, waits for them, and re-layouts  114 us (11%)
  matrix products  91.2 us (9%)
  between operations  19.6 us (2%)
  starting transfers between devices  12.2 us (1%)
    psum x2, waiting for transfers between devices, from_root(): return lax.psum(kept, axis)  203 us
    another operation x30, other arithmetic, shards(): factor = jnp.linalg.cholesky(diag_matrix)  159 us
    all_to_all x1, waiting for transfers between devices, shards(): lax.all_to_all(merged, ('row', 'col'), split_axis=0, concat_axis=0, tiled...  101 us
    all_gather x2, waiting for transfers between devices, shards(): lax.all_gather(panel_rows[low_row:high_row + 1], 'row', axis=0, tiled=True)  98.3 us
    another operation x5, other arithmetic, shards(): lax.linalg.triangular_solve(factor, jnp.eye(panel_width, dtype=jnp.float3...  81.1 us
    all_gather x2, waiting for transfers between devices, shards(): lax.all_gather(front[:, low_col:high_col + 1], 'col', axis=1, tiled=True)  64.7 us
    dot_general x2, matrix products, shards(): jnp.einsum('lxw,myw->lmxy', lower_rows, column_lower, precision=exact_pre...  32.2 us
    scatter-add x1, other arithmetic, shards(): gains.at[target].add(arrived.reshape(-1, edge_size, edge_size), mode='drop')  25.6 us
  transfers between devices with their start and end apart: 7, of which 7 were waited for; matrix products, arithmetic and copies ran while one was open for 1% of the time, Pallas kernels for 0%

commit v1 on v0

v1 whole, which is shorter than its diff:
```python
import jax
import jax.numpy as jnp
from jax import lax
from jax.experimental import pallas as pl
from jax.experimental.pallas import tpu as pltpu
from jax.sharding import PartitionSpec as P

B = 128
HB = 64
ROWS = 16
COLS = 8
HALF = 8
LR = 8
LC = 16
CB = 8
PANEL = 1024
f32 = jnp.float32
bf16 = jnp.bfloat16
exact = lax.Precision.HIGHEST
MIB = 2**20


def block_dot(left, right, contract_left=1):
    dims = (((contract_left,), (0,)), ((), ()))
    return lax.dot_general(left, right, dims, preferred_element_type=f32)


def exact_dot(left, right, contract_left=1):
    dims = (((contract_left,), (0,)), ((), ()))
    return lax.dot_general(left, right, dims, precision=exact, preferred_element_type=f32)


def split(value):
    high = value.astype(bf16)
    return high, (value - high.astype(f32)).astype(bf16)


def slot_first(match, dup):
    return jnp.maximum(jnp.where(match > 0, match, dup) - 1, 0)


def pack_slots(child, table, second):
    def pick(step, tab):
        match = tab[step]
        if second:
            return jnp.maximum(match - 1, 0), 0, 1, 0, 0
        dup = tab[ROWS + step]
        lower = jnp.logical_and(match == 0, dup > 0).astype(jnp.int32)
        return slot_first(match, dup), 0, lower, 0, 0

    def body(tab, child_ref, out_ref):
        step = pl.program_id(0)
        match = tab[step]
        dup = tab[ROWS + step]
        if second:
            used = match > 0
            row = jnp.maximum(match - 1, 0)
        else:
            used = jnp.logical_or(match > 0, dup > 0)
            row = slot_first(match, dup)
        for place in range(COLS):
            source = tab[2 * ROWS + place]
            kept = tab[2 * ROWS + COLS + row * CB + source]
            gain = jnp.where(used, kept, 0).astype(f32)
            out_ref[0, place] = child_ref[0, source, 0] * gain

    return pl.pallas_call(
        body,
        grid_spec=pltpu.PrefetchScalarGridSpec(
            num_scalar_prefetch=1,
            grid=(ROWS,),
            in_specs=[pl.BlockSpec((1, CB, 1, HB, B), pick)],
            out_specs=pl.BlockSpec((1, COLS, HB, B), lambda step, tab: (step, 0, 0, 0)),
        ),
        out_shape=jax.ShapeDtypeStruct((ROWS, COLS, HB, B), f32),
        compiler_params=pltpu.CompilerParams(vmem_limit_bytes=16 * MIB),
        cost_estimate=pl.CostEstimate(flops=2**20, bytes_accessed=8 * MIB, transcendentals=0),
    )(table, child)


def gain_of(code):
    return (code > 0).astype(f32)


def place_of(code):
    return jnp.maximum(code - 1, 0)


NKEYS = LR + 1 + LC


def leading_row(front, received, arrived, table):
    def body(tab, own_ref, recv_ref, first_ref, other_ref, top_ref, even_ref, odd_ref, lead_ref):
        upper = tab[2 * NKEYS] < HALF
        side = tab[2 * NKEYS] // HALF
        for m in range(LC):
            value = jnp.where(upper, own_ref[0, m, 0], recv_ref[m])
            for child, ref in ((0, first_ref), (1, other_ref)):
                base = child * NKEYS
                code = tab[base + LR + 1 + m]
                gain = gain_of(code) * gain_of(tab[base + LR])
                value = value + ref[0, place_of(code)] * gain
            top_ref[m] = value
        lead_ref[...] = top_ref[0]
        for l in range(LR):
            even_ref[l] = top_ref[2 * l + side]
            odd_ref[l] = top_ref[2 * l + 1 - side]

    def rows_of(child):
        return lambda step, tab: (child * HALF + place_of(tab[child * NKEYS + LR]), 0, 0, 0)

    return pl.pallas_call(
        body,
        grid_spec=pltpu.PrefetchScalarGridSpec(
            num_scalar_prefetch=1,
            grid=(1,),
            in_specs=[
                pl.BlockSpec((1, LC, 1, HB, B), lambda step, tab: (0, 0, 0, 0, 0)),
                pl.BlockSpec((LC, HB, B), lambda step, tab: (0, 0, 0)),
                pl.BlockSpec((1, COLS, HB, B), rows_of(0)),
                pl.BlockSpec((1, COLS, HB, B), rows_of(1)),
            ],
            out_specs=[
                pl.BlockSpec((LC, HB, B), lambda step, tab: (0, 0, 0)),
                pl.BlockSpec((LR, HB, B), lambda step, tab: (0, 0, 0)),
                pl.BlockSpec((LR, HB, B), lambda step, tab: (0, 0, 0)),
                pl.BlockSpec((HB, B), lambda step, tab: (0, 0)),
            ],
        ),
        out_shape=[
            jax.ShapeDtypeStruct((LC, HB, B), f32),
            jax.ShapeDtypeStruct((LR, HB, B), f32),
            jax.ShapeDtypeStruct((LR, HB, B), f32),
            jax.ShapeDtypeStruct((HB, B), f32),
        ],
        compiler_params=pltpu.CompilerParams(vmem_limit_bytes=16 * MIB),
        cost_estimate=pl.CostEstimate(flops=2**20, bytes_accessed=3 * MIB, transcendentals=0),
    )(table, front, received, arrived, arrived)


def extend_add(front, arrived, table, half):
    def body(tab, parent_ref, first_ref, other_ref, out_ref):
        step = pl.program_id(0)
        for m in range(LC):
            value = parent_ref[0, m, 0]
            for child, ref in ((0, first_ref), (1, other_ref)):
                base = child * NKEYS
                code = tab[base + LR + 1 + m]
                gain = gain_of(code) * gain_of(tab[base + step])
                value = value + ref[0, place_of(code)] * gain
            out_ref[0, m] = value

    def rows_of(child):
        return lambda step, tab: (child * HALF + place_of(tab[child * NKEYS + step]), 0, 0, 0)

    return pl.pallas_call(
        body,
        grid_spec=pltpu.PrefetchScalarGridSpec(
            num_scalar_prefetch=1,
            grid=(LR,),
            in_specs=[
                pl.BlockSpec((1, LC, 1, HB, B), lambda step, tab: (step, 0, half, 0, 0)),
                pl.BlockSpec((1, COLS, HB, B), rows_of(0)),
                pl.BlockSpec((1, COLS, HB, B), rows_of(1)),
            ],
            out_specs=pl.BlockSpec((1, LC, HB, B), lambda step, tab: (step, 0, 0, 0)),
        ),
        out_shape=jax.ShapeDtypeStruct((LR, LC, HB, B), f32),
        compiler_params=pltpu.CompilerParams(vmem_limit_bytes=16 * MIB),
        cost_estimate=pl.CostEstimate(flops=2**21, bytes_accessed=12 * MIB, transcendentals=0),
    )(table, front, arrived, arrived)


def factor_block(block):
    lane = lax.broadcasted_iota(jnp.int32, (8, B), 1)
    sub = lax.broadcasted_iota(jnp.int32, (8, B), 0)

    def lanes(tile, j):
        return jnp.broadcast_to(tile[:, j : j + 1], (8, B))

    def subs(tile, k):
        return jnp.broadcast_to(tile[k : k + 1, :], (8, B))

    tiles = [block[8 * r : 8 * r + 8, :] for r in range(B // 8)]
    for group in range(B // 8):
        low = 8 * group
        rest = range(group + 1, B // 8)
        own = [lanes(tiles[group], low + k) for k in range(8)]
        far = {r: [lanes(tiles[r], low + k) for k in range(8)] for r in rest}
        inside = jnp.logical_and(lane >= low, lane < low + 8)
        scaled = []
        for k in range(8):
            inv = 1.0 / subs(own[k], k)
            here = lane == low + k
            row = jnp.where(here, 1.0, subs(tiles[group], k)) * inv
            later = jnp.logical_and(lane > low + k, lane < low + 8)
            scaled.append(jnp.where(later, 0.0, row))
            steps = {m: subs(own[m], k) * inv for m in range(k + 1, 8)}
            if k < 7:
                below = sub > k
                coef = jnp.where(below, own[k], 0.0)
                clear = jnp.logical_and(below, here)
                tiles[group] = jnp.where(clear, 0.0, tiles[group]) - coef * row
                for m in range(k + 1, 8):
                    own[m] = own[m] - coef * steps[m]
            for r in rest:
                for m in range(k + 1, 8):
                    far[r][m] = far[r][m] - far[r][k] * steps[m]
        for r in rest:
            value = jnp.where(inside, 0.0, tiles[r])
            for k in range(8):
                value = value - far[r][k] * scaled[k]
            tiles[r] = value
    return jnp.concatenate(tiles, axis=0)


def leading_factor(pieces, where):
    def body(at, *refs):
        piece_refs, (w, diag) = refs[:8], refs[8:]
        for n, ref in enumerate(piece_refs):
            dk, dy = n // 4, n % 4
            q = ((at[2] + dy) % 4) * 2 + (at[3] + dk) % 2
            for dx in range(4):
                x = (at[0] + dx) % 4
                for dz in range(4):
                    g = (x % 2) * 4 + (at[1] + dz) % 4
                    top = pl.multiple_of(g * B + (x // 2) * HB, HB)
                    w[pl.ds(top, HB), pl.ds(pl.multiple_of(q * B, B), B)] = ref[dx, dz]
        row = lax.broadcasted_iota(jnp.int32, (B, B), 0)
        col = lax.broadcasted_iota(jnp.int32, (B, B), 1)

        def step(kb, carry):
            o = pl.multiple_of(kb * B, B)
            f = factor_block(w[pl.ds(o, B), pl.ds(o, B)])
            pivots = jnp.sum(jnp.where(row == col, f, 0.0), axis=1, keepdims=True)
            scale = 1.0 / jnp.sqrt(pivots)
            inverse = jnp.where(row > col, f, (row == col).astype(f32)) * scale
            diag[pl.ds(o, B), :] = jnp.where(row <= col, f, 0.0) * scale
            w[pl.ds(o, B), :] = exact_dot(inverse, w[pl.ds(o, B), :])
            w[pl.ds(o, B), pl.ds(o, B)] = inverse

            @pl.when(kb % 2 == 0)
            def _():
                n = pl.multiple_of(o + B, B)
                w[pl.ds(n, B), pl.ds(o, B)] = jnp.zeros((B, B), f32)
                w[pl.ds(n, B), :] -= exact_dot(w[pl.ds(o, B), pl.ds(n, B)], w[pl.ds(o, B), :], 0)

            for done in range(256, PANEL, 256):

                @pl.when(kb == done // B - 1)
                def _():
                    above = (slice(done - 256, done - B), slice(done - B, done))
                    kept = w[above]
                    w[above] = jnp.zeros((B, B), f32)
                    w[done:, done - 256 : done] = jnp.zeros((PANEL - done, 256), f32)
                    for n in range(done, PANEL, 256):
                        left = w[done - 256 : done, n : n + 256]
                        w[n : n + 256, :] -= exact_dot(left, w[done - 256 : done, :], 0)
                    w[above] = kept

            return carry

        lax.fori_loop(0, PANEL // B, step, 0)

    return pl.pallas_call(
        body,
        in_specs=[pl.BlockSpec(memory_space=pltpu.SMEM)]
        + [pl.BlockSpec(memory_space=pltpu.VMEM)] * 8,
        out_specs=[pl.BlockSpec(memory_space=pltpu.VMEM)] * 2,
        out_shape=[
            jax.ShapeDtypeStruct((PANEL, PANEL), f32),
            jax.ShapeDtypeStruct((PANEL, B), f32),
        ],
        compiler_params=pltpu.CompilerParams(vmem_limit_bytes=40 * MIB),
        cost_estimate=pl.CostEstimate(
            flops=50 * 2**30, bytes_accessed=9 * MIB, transcendentals=1024
        ),
    )(where, *pieces)


def panel_solve(rows, w, diag, where):
    def body(at, rows_ref, w_ref, diag_ref, high_ref, low_ref, out_ref, gh, gl, wh, wl, bt, bh, bl):
        p, q = at[0], at[1]
        side = p // HALF
        for e in range(COLS):
            for order in range(2):
                half = side if order == 0 else 1 - side
                top = pl.multiple_of(e * B + half * HB, HB)
                for l in range(LR):
                    high, low = split(rows_ref[e, order, l])
                    gh[pl.ds(top, HB), l * B : (l + 1) * B] = high
                    gl[pl.ds(top, HB), l * B : (l + 1) * B] = low
        for r in range(0, PANEL, 256):
            shape = (256, r + 256)
            under = (
                lax.broadcasted_iota(jnp.int32, shape, 0) + r
                >= lax.broadcasted_iota(jnp.int32, shape, 1)
            )
            high, low = split(jnp.where(under, w_ref[r : r + 256, : r + 256], 0.0))
            wh[r : r + 256, : r + 256] = high
            wl[r : r + 256, : r + 256] = low
            value = block_dot(high, gh[: r + 256, :])
            value += block_dot(high, gl[: r + 256, :])
            value += block_dot(low, gh[: r + 256, :])
            bt[r : r + 256, :] = value
            high, low = split(value)
            bh[r : r + 256, :] = high
            bl[r : r + 256, :] = low
        mine = pl.ds(pl.multiple_of(q * B, B), B)
        for l in range(LR):
            out_ref[l] = bt[mine, l * B : (l + 1) * B].T

        @pl.when(p < HALF)
        def _():
            over = w_ref[mine, pl.ds(pl.multiple_of((p % HALF) * B, B), B)]
            top = jnp.where(p > q, over, jnp.where(p == q, diag_ref[mine, :], 0.0))
            out_ref[0] = top.T

        for r in range(0, PANEL, 256):
            value = block_dot(wh[r:, r : r + 256], bh[r:, :], 0)
            value += block_dot(wh[r:, r : r + 256], bl[r:, :], 0)
            value += block_dot(wl[r:, r : r + 256], bh[r:, :], 0)
            for l in range(LR):
                for n in range(0, 256, B):
                    high, low = split(value[n : n + B, l * B : (l + 1) * B].T)
                    high_ref[l * B : (l + 1) * B, r + n : r + n + B] = high
                    low_ref[l * B : (l + 1) * B, r + n : r + n + B] = low

        @pl.when(p < HALF)
        def _():
            high_ref[:B, :] = jnp.zeros((B, PANEL), bf16)
            low_ref[:B, :] = jnp.zeros((B, PANEL), bf16)

    return pl.pallas_call(
        body,
        in_specs=[pl.BlockSpec(memory_space=pltpu.SMEM)]
        + [pl.BlockSpec(memory_space=pltpu.VMEM)] * 3,
        out_specs=[pl.BlockSpec(memory_space=pltpu.VMEM)] * 3,
        out_shape=[
            jax.ShapeDtypeStruct((PANEL, PANEL), bf16),
            jax.ShapeDtypeStruct((PANEL, PANEL), bf16),
            jax.ShapeDtypeStruct((LR, B, B), f32),
        ],
        scratch_shapes=[
            pltpu.VMEM((PANEL, PANEL), bf16),
            pltpu.VMEM((PANEL, PANEL), bf16),
            pltpu.VMEM((PANEL, PANEL), bf16),
            pltpu.VMEM((PANEL, PANEL), bf16),
            pltpu.VMEM((PANEL, PANEL), f32),
            pltpu.VMEM((PANEL, PANEL), bf16),
            pltpu.VMEM((PANEL, PANEL), bf16),
        ],
        compiler_params=pltpu.CompilerParams(vmem_limit_bytes=48 * MIB),
        cost_estimate=pl.CostEstimate(
            flops=8 * 2**30, bytes_accessed=14 * MIB, transcendentals=0
        ),
    )(where, rows, w, diag)


def trailing_update(upper, lower, columns, high, low, panel):
    def body(upper_ref, lower_ref, col_ref, high_ref, low_ref, panel_ref, out_ref, ch, cl):
        for p in range(ROWS):
            top = (p % HALF) * B + (p // HALF) * HB
            for n in range(2):
                hi, lo = split(col_ref[p, n])
                ch[top : top + HB, n * B : (n + 1) * B] = hi
                cl[top : top + HB, n * B : (n + 1) * B] = lo
        for r in range(0, PANEL, 256):
            value = block_dot(high_ref[r : r + 256, :], ch[...])
            value += block_dot(high_ref[r : r + 256, :], cl[...])
            value += block_dot(low_ref[r : r + 256, :], ch[...])
            for l in range(r // B, r // B + 2):
                for n in range(2):
                    s = l * B - r
                    cols = slice(n * B, (n + 1) * B)
                    out_ref[l, n, :HB] = upper_ref[l, n] - value[s : s + HB, cols]
                    out_ref[l, n, HB:] = lower_ref[l, n] - value[s + HB : s + B, cols]

        @pl.when(pl.program_id(0) == 0)
        def _():
            for l in range(LR):
                out_ref[l, 0] = panel_ref[l]

    half = pl.BlockSpec((LR, 2, HB, B), lambda step: (0, step, 0, 0))
    whole = pl.BlockSpec((PANEL, PANEL), lambda step: (0, 0))
    return pl.pallas_call(
        body,
        grid=(LC // 2,),
        in_specs=[
            half,
            half,
            pl.BlockSpec((ROWS, 2, HB, B), lambda step: (0, step, 0, 0)),
            whole,
            whole,
            pl.BlockSpec((LR, B, B), lambda step: (0, 0, 0)),
        ],
        out_specs=pl.BlockSpec((LR, 2, B, B), lambda step: (0, step, 0, 0)),
        out_shape=jax.ShapeDtypeStruct((LR, LC, B, B), f32),
        scratch_shapes=[pltpu.VMEM((PANEL, 256), bf16), pltpu.VMEM((PANEL, 256), bf16)],
        compiler_params=pltpu.CompilerParams(vmem_limit_bytes=40 * MIB),
        cost_estimate=pl.CostEstimate(
            flops=12 * 2**30, bytes_accessed=28 * MIB, transcendentals=0
        ),
    )(upper, lower, columns, high, low, panel)


def along_x(distance):
    return [(4 * ((x + distance) % 4) + z, 4 * x + z) for x in range(4) for z in range(4)]


def along_z(distance):
    return [(4 * x + (z + distance) % 4, 4 * x + z) for x in range(4) for z in range(4)]


def along_y(distance):
    return [(2 * ((y + distance) % 4) + k, 2 * y + k) for y in range(4) for k in range(2)]


OTHER_CORE = [(q, q ^ 1) for q in range(COLS)]


def transposed(same):
    pairs = []
    for p in range(ROWS):
        for q in range(COLS):
            side = p // HALF if same else 1 - p // HALF
            pairs.append((p * COLS + q, (q + HALF * side) * COLS + p % HALF))
    return pairs


def shards(parent_front, child_updates, child_mask, child_map):
    p = lax.axis_index("row")
    q = lax.axis_index("col")
    both = ("row", "col")
    front = parent_front.reshape(LR, LC, 2, HB, B)
    child = child_updates.reshape(CB, CB, 2, HB, B)

    own_map = child_map[p // HALF].reshape(CB, CB)
    row_parent = own_map[:, p % HALF]
    col_parent = own_map[:, q]
    index = jnp.arange(CB)
    slots = jnp.arange(ROWS)
    match = jnp.sum((row_parent[None] % ROWS == slots[:, None]) * (index + 1)[None], axis=1)
    dup = jnp.sum((row_parent[None] + HALF == slots[:, None]) * (index + 1)[None], axis=1)
    column = jnp.sum((col_parent[None] % COLS == index[:, None]) * index[None], axis=1)
    source_table = jnp.concatenate([match, dup, column, child_mask.reshape(-1)]).astype(jnp.int32)

    keys = jnp.concatenate(
        [jnp.arange(LR) * ROWS + p, (p % HALF)[None], jnp.arange(LC) * COLS + q]
    )
    hits = child_map[:, None, :] == keys[None, :, None]
    codes = jnp.sum(hits * (jnp.arange(CB * CB) % CB + 1)[None, None], axis=2)
    target_table = jnp.concatenate([codes.reshape(-1), p[None]]).astype(jnp.int32)

    top_other = lax.ppermute(front[0, :, 1], "row", [(i, i + HALF) for i in range(HALF)])

    first = pack_slots(child, source_table, False)
    first = lax.all_to_all(
        first.reshape(ROWS * COLS, HB, B), both, 0, 0, tiled=True
    ).reshape(ROWS, COLS, HB, B)
    second = pack_slots(child, source_table, True)

    top, even, odd, lead = leading_row(front, top_other, first, target_table)

    near = [lead] + [lax.ppermute(lead, "row", along_z(d)) for d in range(1, 4)]
    stacked = jnp.stack(near)
    near = [stacked] + [lax.ppermute(stacked, "row", along_x(d)) for d in range(1, 4)]
    stacked = jnp.stack(near)
    near = [stacked] + [lax.ppermute(stacked, "col", along_y(d)) for d in range(1, 4)]
    near = near + [lax.ppermute(piece, "col", OTHER_CORE) for piece in near]

    turned = jnp.stack(
        [lax.ppermute(even, both, transposed(True)), lax.ppermute(odd, both, transposed(False))]
    )
    panel_rows = lax.all_gather(turned, "col", axis=0)
    columns = lax.all_gather(top, "row", axis=0)

    second = lax.all_to_all(
        second.reshape(ROWS * COLS, HB, B), both, 0, 0, tiled=True
    ).reshape(ROWS, COLS, HB, B)
    upper = extend_add(front, first, target_table, 0)

    where = jnp.stack([p // 4, p % 4, q // 2, q % 2]).astype(jnp.int32)
    w, diag = leading_factor(near, where)
    high, low, panel = panel_solve(panel_rows, w, diag, jnp.stack([p, q]).astype(jnp.int32))
    lower = extend_add(front, second, target_table, 1)
    return trailing_update(upper, lower, columns, high, low, panel)


def solution(mesh):
    in_specs = (P("row", "col", None, None), P("row", "col", None, None), P("row", "col"), P())
    out_specs = P("row", "col", None, None)
    return jax.shard_map(shards, mesh=mesh, in_specs=in_specs, out_specs=out_specs, check_vma=False)
```

time: 1030 us -> 341 us (0.33)
  waiting for transfers between devices: 467 us -> 117 us
  other arithmetic: 323 us -> 2.08 us
  Pallas kernels: 0 us -> 96.6 us
  matrix products: 91.2 us -> 0 us
  local copies, waits for them, and re-layouts: 114 us -> 37.1 us
  starting transfers between devices: 12.2 us -> 73.4 us
    another operation x39 -> x5, other arithmetic: 251 us -> 1.03 us  [the longest x1 0.83 us: shards(): jnp.stack([lax.ppermute(even, both, transposed(True)), lax.ppermute(odd,...]
    psum x2 -> x0, waiting for transfers between devices: 203 us -> none  [from_root(): return lax.psum(kept, axis)]
    all_gather x4 -> x2, waiting for transfers between devices: 163 us -> 0.01 us  [the longest x1 0.01 us: shards(): panel_rows = lax.all_gather(turned, 'col', axis=0)]
    ppermute x0 -> x16, waiting for transfers between devices: none -> 116 us  [the longest x1 47.5 us: shards(): lax.ppermute(front[0, :, 1], 'row', [(i, i + HALF) for i in range(HALF)])]
    all_to_all x1 -> x2, waiting for transfers between devices: 101 us -> 0.01 us  [the longest x1 0.01 us: shards(): lax.all_to_all(second.reshape(ROWS * COLS, HB, B), both, 0, 0, tiled=True)]
    pallas_call x0 -> x8, Pallas kernels: none -> 96.6 us  [the longest x1 48.1 us: leading_factor(): pl.pallas_call(body, in_specs=[pl.BlockSpec(memory_space=pltpu.SMEM)] + [...]
    dot_general x6 -> x0, matrix products: 67.6 us -> none  [the longest x2 32.2 us: shards(): jnp.einsum('lxw,myw->lmxy', lower_rows, column_lower, precision=exact_pre...]
    scatter-add x2 -> x0, other arithmetic: 39.5 us -> none  [the longest x1 25.6 us: shards(): gains.at[target].add(arrived.reshape(-1, edge_size, edge_size), mode='drop')]
  transfers between devices with their start and end apart: 7 -> 20, of which waited for: 7 -> 11; matrix products, arithmetic and copies ran while one was open for 1% -> 1% of each run, Pallas kernels for 0% -> 22%
where the time goes in v1:
time: 341 us; the launch traced here: 340 us
  waiting for transfers between devices  117 us (34%)
  Pallas kernels  96.6 us (28%)
  starting transfers between devices  73.4 us (22%)
  local copies, waits for them, and re-layouts  37.1 us (11%)
  between operations  13.6 us (4%)
    pallas_call x1, Pallas kernels, leading_factor(): pl.pallas_call(body, in_specs=[pl.BlockSpec(memory_space=pltpu.SMEM)] + [...  48.1 us
    ppermute x1, waiting for transfers between devices, shards(): lax.ppermute(front[0, :, 1], 'row', [(i, i + HALF) for i in range(HALF)])  47.5 us
    unnamed x34, local copies, waits for them, and re-layouts  34.1 us
    all_to_all x1, starting transfers between devices, shards(): lax.all_to_all(second.reshape(ROWS * COLS, HB, B), both, 0, 0, tiled=True)  27.2 us
    ppermute x3, waiting for transfers between devices, shards(): lax.ppermute(stacked, 'row', along_x(d))  25.7 us
    ppermute x3, waiting for transfers between devices, shards(): lax.ppermute(stacked, 'col', along_y(d))  22.3 us
    pallas_call x1, Pallas kernels, trailing_update(): pl.pallas_call(body, grid=(LC // 2,), in_specs=[half, half, pl.BlockSpec(...  17.9 us
    ppermute x3, waiting for transfers between devices, shards(): near = [lead] + [lax.ppermute(lead, 'row', along_z(d)) for d in range(1, 4)]  14.8 us
  transfers between devices with their start and end apart: 20, of which 11 were waited for; matrix products, arithmetic and copies ran while one was open for 1% of the time, Pallas kernels for 22%

profile of v1, /device:TPU:1, one launch (start us, length us, event | category | flops | bytes accessed | tf_op | source)
XLA Modules:
  0.0 340.0 jit_solution(9814938047539738296)
XLA Ops:
  8.6 2.2 copy-done.3
  14.6 12.0 %all-to-all-start = ((f32[128,64,128]{2,1,0:T(8,128)}), f32[128,64,128]{2,1,0:T(8,128)}, u32[]{:S(2)}, u32[]{:S(2)}) async-start(f32[128,64,128]{2,1,0:T(8,128)} %bitcast.37), calls=%async_computation | async-start | bytes 8388608 | tf_op jit(solution)/shard_map/all_to_all | solution.py:458
  27.7 4.8 %collective-permute-start = (f32[16,64,128]{2,1,0:T(8,128)S(1)}, f32[16,64,128]{2,1,0:T(8,128)S(1)}, u32[]{:S(2)}, u32[]{:S(2)}) collective-permute-start(f32[16,64,128]{2,1,0:T(8,128)S(1)} %slice_bitcast_fusion), channel_id=1, source_target_pairs={{0,64},{8,72},{16,80},{24,88},{32,96},{40,104},{48,112},{56,120},{... | collective-permute-start | bytes 1572872 | tf_op jit(solution)/shard_map/ppermute | solution.py:455
  33.5 47.5 %collective-permute-done.recv_ref = f32[16,64,128]{2,1,0:T(8,128)S(1)} collective-permute-done((f32[16,64,128]{2,1,0:T(8,128)S(1)}, f32[16,64,128]{2,1,0:T(8,128)S(1)}, u32[]{:S(2)}, u32[]{:S(2)}) %collective-permute-start) | collective-permute-done | bytes 524320 | tf_op jit(solution)/shard_map/ppermute | solution.py:455
  81.0 3.4 copy-done
  84.4 2.6 shard_map.50
  87.0 5.3 %collective-permute-start.1 = (f32[8,64,128]{2,1,0:T(8,128)S(1)}, f32[8,64,128]{2,1,0:T(8,128)S(1)}, u32[]{:S(2)}, u32[]{:S(2)}) collective-permute-start(f32[8,64,128]{2,1,0:T(8,128)S(1)} %get-tuple-element.15), channel_id=1, source_target_pairs={{0,0},{1,8},{2,16},{3,24},{4,32},{5,40},{6,48},{7,56},{8,1},{9,9},... | collective-permute-start | bytes 786440 | tf_op jit(solution)/shard_map/ppermute | solution.py:473
  92.3 3.5 %collective-permute-start.2 = (f32[8,64,128]{2,1,0:T(8,128)S(1)}, f32[8,64,128]{2,1,0:T(8,128)S(1)}, u32[]{:S(2)}, u32[]{:S(2)}) collective-permute-start(f32[8,64,128]{2,1,0:T(8,128)S(1)} %get-tuple-element.16), channel_id=1, source_target_pairs={{0,64},{1,72},{2,80},{3,88},{4,96},{5,104},{6,112},{7,120},{8,65},... | collective-permute-start | bytes 786440 | tf_op jit(solution)/shard_map/ppermute | solution.py:473
  95.8 2.0 collective-permute-done.1
  97.8 4.1 %collective-permute-done.2 = f32[8,64,128]{2,1,0:T(8,128)S(1)} collective-permute-done((f32[8,64,128]{2,1,0:T(8,128)S(1)}, f32[8,64,128]{2,1,0:T(8,128)S(1)}, u32[]{:S(2)}, u32[]{:S(2)}) %collective-permute-start.2) | collective-permute-done | bytes 262176 | tf_op jit(solution)/shard_map/ppermute | solution.py:473
  103.6 2.2 copy-done.4
  107.3 2.0 copy-done.5
  109.4 27.2 %all-to-all-start.1 = ((f32[128,64,128]{2,1,0:T(8,128)}), f32[128,64,128]{2,1,0:T(8,128)}, u32[]{:S(2)}, u32[]{:S(2)}) async-start(f32[128,64,128]{2,1,0:T(8,128)} %bitcast.36), calls=%async_computation.1 | async-start | bytes 8388608 | tf_op jit(solution)/shard_map/all_to_all | solution.py:478
  136.5 3.3 collective-permute-start.3
  140.8 12.4 %collective-permute-done.3 = f32[64,128]{1,0:T(8,128)S(1)} collective-permute-done((f32[64,128]{1,0:T(8,128)S(1)}, f32[64,128]{1,0:T(8,128)S(1)}, u32[]{:S(2)}, u32[]{:S(2)}) %collective-permute-start.3) | collective-permute-done | bytes 32800 | tf_op jit(solution)/shard_map/ppermute | solution.py:465
  153.2 2.4 collective-permute-done.5
  155.6 4.7 %collective-permute-start.6 = (f32[4,64,128]{2,1,0:T(8,128)S(1)}, f32[4,64,128]{2,1,0:T(8,128)S(1)}, u32[]{:S(2)}, u32[]{:S(2)}) collective-permute-start(f32[4,64,128]{2,1,0:T(8,128)S(1)} %get-tuple-element.28), channel_id=1, source_target_pairs={{32,0},{40,8},{48,16},{56,24},{64,32},{72,40},{80,48},{88,56},{96,... | collective-permute-start | bytes 393224 | tf_op jit(solution)/shard_map/ppermute | solution.py:467
  160.3 2.9 collective-permute-start.7
  163.9 21.5 %collective-permute-done.6 = f32[4,64,128]{2,1,0:T(8,128)S(1)} collective-permute-done((f32[4,64,128]{2,1,0:T(8,128)S(1)}, f32[4,64,128]{2,1,0:T(8,128)S(1)}, u32[]{:S(2)}, u32[]{:S(2)}) %collective-permute-start.6) | collective-permute-done | bytes 131104 | tf_op jit(solution)/shard_map/ppermute | solution.py:467
  186.9 2.7 collective-permute-done.8
  189.6 2.4 collective-permute-start.9
  194.8 12.5 %collective-permute-done.9.refs_1_ = f32[4,4,64,128]{3,2,1,0:T(8,128)S(1)} collective-permute-done((f32[4,4,64,128]{3,2,1,0:T(8,128)S(1)}, f32[4,4,64,128]{3,2,1,0:T(8,128)S(1)}, u32[]{:S(2)}, u32[]{:S(2)}) %collective-permute-start.9) | collective-permute-done | bytes 524320 | tf_op jit(solution)/shard_map/ppermute | solution.py:469
  209.5 9.7 %collective-permute-done.11.refs_3_ = f32[4,4,64,128]{3,2,1,0:T(8,128)S(1)} collective-permute-done((f32[4,4,64,128]{3,2,1,0:T(8,128)S(1)}, f32[4,4,64,128]{3,2,1,0:T(8,128)S(1)}, u32[]{:S(2)}, u32[]{:S(2)}) %collective-permute-start.11) | collective-permute-done | bytes 524320 | tf_op jit(solution)/shard_map/ppermute | solution.py:469
  220.1 3.7 %copy-done.1 = f32[8,16,128,128]{3,2,1,0:T(8,128)S(1)} copy-done((f32[8,16,128,128]{3,2,1,0:T(8,128)S(1)}, f32[8,16,128,128]{3,2,1,0:T(8,128)}, u32[]{:S(2)}) %copy-start.1) | copy-done | bytes 8388632
  223.8 5.6 %shard_map.47.upper_ref = f32[8,16,64,128]{3,2,1,0:T(8,128)S(1)} custom-call(s32[51]{0:T(128)S(1)} %pad_add_fusion.1.tab, f32[8,16,2,64,128]{4,3,2,1,0:T(8,128)S(1)} %bitcast.32, f32[16,8,64,128]{3,2,1,0:T(8,128)} %bitcast.5.first_ref.other_ref, f32[16,8,64,128]{3,2,1,0:T(8,128)} %bitcast.5.first_ref.other_ref), custom_call_target="tpu_custom_call" | custom-call | flops 2097152 | bytes 12582912 | tf_op jit(solution)/shard_map/pallas_call | solution.py:156
  231.5 3.5 %copy-done.2 = f32[8,16,128,128]{3,2,1,0:T(8,128)S(1)} copy-done((f32[8,16,128,128]{3,2,1,0:T(8,128)S(1)}, f32[8,16,128,128]{3,2,1,0:T(8,128)}, u32[]{:S(2)}) %copy-start.2) | copy-done | bytes 8388632
  235.0 5.6 %shard_map.49.lower_ref = f32[8,16,64,128]{3,2,1,0:T(8,128)S(1)} custom-call(s32[51]{0:T(128)S(1)} %pad_add_fusion.1.tab, f32[8,16,2,64,128]{4,3,2,1,0:T(8,128)S(1)} %bitcast.33, f32[16,8,64,128]{3,2,1,0:T(8,128)} %bitcast.7.first_ref.other_ref, f32[16,8,64,128]{3,2,1,0:T(8,128)} %bitcast.7.first_ref.other_ref), custom_call_target="tpu_custom_call" | custom-call | flops 2097152 | bytes 12582912 | tf_op jit(solution)/shard_map/pallas_call | solution.py:156
  242.6 48.1 %shard_map.51 = (f32[1024,1024]{1,0:T(8,128)S(1)}, f32[1024,128]{1,0:T(8,128)S(1)}) custom-call(s32[4]{0:T(128)S(1)} %pad_add_fusion.4.at, f32[4,4,64,128]{3,2,1,0:T(8,128)S(1)} %pad_maximum_fusion.1.refs_0_, f32[4,4,64,128]{3,2,1,0:T(8,128)S(1)} %collective-permute-done.9.refs_1_, f32[4,4,64,128]{3,2,1,0:T(8,128)S(1)} %collective-permute-done.10.refs_2_, ...), custom_call_target="tpu_custom_call" | custom-call | flops 53687091200 | bytes 9437184 | tf_op jit(solution)/shard_map/pallas_call | solution.py:265
  294.4 13.4 %shard_map.52 = (bf16[1024,1024]{1,0:T(8,128)(2,1)S(1)}, bf16[1024,1024]{1,0:T(8,128)(2,1)S(1)}, f32[8,128,128]{2,1,0:T(8,128)S(1)}) custom-call(s32[2]{0:T(128)S(1)} %pad_add_fusion.3.at, f32[8,2,8,64,128]{4,3,2,1,0:T(8,128)} %bitcast.48, f32[1024,1024]{1,0:T(8,128)} %copy-done.11, f32[1024,128]{1,0:T(8,128)S(1)} %copy-done.15), custom_call_target="tpu_custom_call" | custom-call | flops 8589934592 | bytes 14680064 | tf_op jit(solution)/shard_map/pallas_call | solution.py:334
  309.2 2.2 copy-done.8
  311.4 2.2 copy-done.10
  315.2 17.9 %shard_map.53 = f32[8,16,128,128]{3,2,1,0:T(8,128)} custom-call(f32[8,16,64,128]{3,2,1,0:T(8,128)S(1)} %copy-done.8, f32[8,16,64,128]{3,2,1,0:T(8,128)S(1)} %copy-done.10, f32[16,16,64,128]{3,2,1,0:T(8,128)} %bitcast.47, bf16[1024,1024]{1,0:T(8,128)(2,1)S(1)} %get-tuple-element.20.high_ref, bf16[1024,1024]{1,0:T(8,128)(2,1)S(1)} %copy-done.13, ...), custom_call_target="tpu_custom_call" | custom-call | flops 12884901888 | bytes 29360128 | tf_op jit(solution)/shard_map/pallas_call | solution.py:386
  (75 shorter events, 30.8 us)
Async XLA Ops:
  8.6 2.2 copy-start.3
  12.6 2.0 copy-start.6
  14.6 18.1 %copy-start.16 = (s32[2,64]{1,0:T(2,128)S(1)}, s32[2,64]{1,0:T(2,128)}, u32[]{:S(2)}) copy-start(s32[2,64]{1,0:T(2,128)} %param.7) | copy-start | bytes 1540
  14.6 66.5 %all-to-all-start = ((f32[128,64,128]{2,1,0:T(8,128)}), f32[128,64,128]{2,1,0:T(8,128)}, u32[]{:S(2)}, u32[]{:S(2)}) async-start(f32[128,64,128]{2,1,0:T(8,128)} %bitcast.37), calls=%async_computation | async-start | bytes 8388608 | tf_op jit(solution)/shard_map/all_to_all | solution.py:458
  26.6 266.8 %all-gather.7.cloned.1.call-start = ((), (), s32[]{:S(2)}) async-start(), calls=%async_computation.3 | async-start | bytes 4718592 | tf_op jit(solution)/shard_map/all_gather | solution.py:475
  27.7 53.3 %collective-permute-start = (f32[16,64,128]{2,1,0:T(8,128)S(1)}, f32[16,64,128]{2,1,0:T(8,128)S(1)}, u32[]{:S(2)}, u32[]{:S(2)}) collective-permute-start(f32[16,64,128]{2,1,0:T(8,128)S(1)} %slice_bitcast_fusion), channel_id=1, source_target_pairs={{0,64},{8,72},{16,80},{24,88},{32,96},{40,104},{48,112},{56,120},{... | collective-permute-start | bytes 1572872 | tf_op jit(solution)/shard_map/ppermute | solution.py:455
  81.0 3.4 copy-start
  87.0 10.8 %collective-permute-start.1 = (f32[8,64,128]{2,1,0:T(8,128)S(1)}, f32[8,64,128]{2,1,0:T(8,128)S(1)}, u32[]{:S(2)}, u32[]{:S(2)}) collective-permute-start(f32[8,64,128]{2,1,0:T(8,128)S(1)} %get-tuple-element.15), channel_id=1, source_target_pairs={{0,0},{1,8},{2,16},{3,24},{4,32},{5,40},{6,48},{7,56},{8,1},{9,9},... | collective-permute-start | bytes 786440 | tf_op jit(solution)/shard_map/ppermute | solution.py:473
  92.3 9.7 %collective-permute-start.2 = (f32[8,64,128]{2,1,0:T(8,128)S(1)}, f32[8,64,128]{2,1,0:T(8,128)S(1)}, u32[]{:S(2)}, u32[]{:S(2)}) collective-permute-start(f32[8,64,128]{2,1,0:T(8,128)S(1)} %get-tuple-element.16), channel_id=1, source_target_pairs={{0,64},{1,72},{2,80},{3,88},{4,96},{5,104},{6,112},{7,120},{8,65},... | collective-permute-start | bytes 786440 | tf_op jit(solution)/shard_map/ppermute | solution.py:473
  102.8 206.4 %all-gather.5.cloned.1.call-start = ((), (), s32[]{:S(2)}) async-start(), calls=%async_computation.2 | async-start | bytes 8912896 | tf_op jit(solution)/shard_map/all_gather | solution.py:476
  103.5 2.2 copy-start.4
  107.3 2.0 copy-start.5
  109.4 122.1 %all-to-all-start.1 = ((f32[128,64,128]{2,1,0:T(8,128)}), f32[128,64,128]{2,1,0:T(8,128)}, u32[]{:S(2)}, u32[]{:S(2)}) async-start(f32[128,64,128]{2,1,0:T(8,128)} %bitcast.36), calls=%async_computation.1 | async-start | bytes 8388608 | tf_op jit(solution)/shard_map/all_to_all | solution.py:478
  136.5 16.6 %collective-permute-start.3 = (f32[64,128]{1,0:T(8,128)S(1)}, f32[64,128]{1,0:T(8,128)S(1)}, u32[]{:S(2)}, u32[]{:S(2)}) collective-permute-start(f32[64,128]{1,0:T(8,128)S(1)} %get-tuple-element.17), channel_id=1, source_target_pairs={{8,0},{16,8},{24,16},{0,24},{40,32},{48,40},{56,48},{32,56},{72,64... | collective-permute-start | bytes 98312 | tf_op jit(solution)/shard_map/ppermute | solution.py:465
  139.9 13.3 %collective-permute-start.4 = (f32[64,128]{1,0:T(8,128)S(1)}, f32[64,128]{1,0:T(8,128)S(1)}, u32[]{:S(2)}, u32[]{:S(2)}) collective-permute-start(f32[64,128]{1,0:T(8,128)S(1)} %get-tuple-element.17), channel_id=1, source_target_pairs={{16,0},{24,8},{0,16},{8,24},{48,32},{56,40},{32,48},{40,56},{80,64... | collective-permute-start | bytes 98312 | tf_op jit(solution)/shard_map/ppermute | solution.py:465
  140.0 15.6 %collective-permute-start.5 = (f32[64,128]{1,0:T(8,128)S(1)}, f32[64,128]{1,0:T(8,128)S(1)}, u32[]{:S(2)}, u32[]{:S(2)}) collective-permute-start(f32[64,128]{1,0:T(8,128)S(1)} %get-tuple-element.17), channel_id=1, source_target_pairs={{24,0},{0,8},{8,16},{16,24},{56,32},{32,40},{40,48},{48,56},{88,64... | collective-permute-start | bytes 98312 | tf_op jit(solution)/shard_map/ppermute | solution.py:465
  155.6 29.9 %collective-permute-start.6 = (f32[4,64,128]{2,1,0:T(8,128)S(1)}, f32[4,64,128]{2,1,0:T(8,128)S(1)}, u32[]{:S(2)}, u32[]{:S(2)}) collective-permute-start(f32[4,64,128]{2,1,0:T(8,128)S(1)} %get-tuple-element.28), channel_id=1, source_target_pairs={{32,0},{40,8},{48,16},{56,24},{64,32},{72,40},{80,48},{88,56},{96,... | collective-permute-start | bytes 393224 | tf_op jit(solution)/shard_map/ppermute | solution.py:467
  160.3 26.6 %collective-permute-start.7 = (f32[4,64,128]{2,1,0:T(8,128)S(1)}, f32[4,64,128]{2,1,0:T(8,128)S(1)}, u32[]{:S(2)}, u32[]{:S(2)}) collective-permute-start(f32[4,64,128]{2,1,0:T(8,128)S(1)} %get-tuple-element.28), channel_id=1, source_target_pairs={{64,0},{72,8},{80,16},{88,24},{96,32},{104,40},{112,48},{120,56},{... | collective-permute-start | bytes 393224 | tf_op jit(solution)/shard_map/ppermute | solution.py:467
  163.2 26.4 %collective-permute-start.8 = (f32[4,64,128]{2,1,0:T(8,128)S(1)}, f32[4,64,128]{2,1,0:T(8,128)S(1)}, u32[]{:S(2)}, u32[]{:S(2)}) collective-permute-start(f32[4,64,128]{2,1,0:T(8,128)S(1)} %get-tuple-element.28), channel_id=1, source_target_pairs={{96,0},{104,8},{112,16},{120,24},{0,32},{8,40},{16,48},{24,56},{32... | collective-permute-start | bytes 393224 | tf_op jit(solution)/shard_map/ppermute | solution.py:467
  189.6 17.6 %collective-permute-start.9 = (f32[4,4,64,128]{3,2,1,0:T(8,128)S(1)}, f32[4,4,64,128]{3,2,1,0:T(8,128)S(1)}, u32[]{:S(2)}, u32[]{:S(2)}) collective-permute-start(f32[4,4,64,128]{3,2,1,0:T(8,128)S(1)} %pad_maximum_fusion.1.refs_0_), channel_id=1, source_target_pairs={{2,0},{3,1},{4,2},{5,3},{6,4},{7,5},{0,6},{1,7},{10,8},{11,9},{12,... | collective-permute-start | bytes 1572872 | tf_op jit(solution)/shard_map/ppermute | solution.py:469
  192.1 16.0 %collective-permute-start.10 = (f32[4,4,64,128]{3,2,1,0:T(8,128)S(1)}, f32[4,4,64,128]{3,2,1,0:T(8,128)S(1)}, u32[]{:S(2)}, u32[]{:S(2)}) collective-permute-start(f32[4,4,64,128]{3,2,1,0:T(8,128)S(1)} %pad_maximum_fusion.1.refs_0_), channel_id=1, source_target_pairs={{4,0},{5,1},{6,2},{7,3},{0,4},{1,5},{2,6},{3,7},{12,8},{13,9},{14,... | collective-permute-start | bytes 1572872 | tf_op jit(solution)/shard_map/ppermute | solution.py:469
  192.5 26.6 %collective-permute-start.11 = (f32[4,4,64,128]{3,2,1,0:T(8,128)S(1)}, f32[4,4,64,128]{3,2,1,0:T(8,128)S(1)}, u32[]{:S(2)}, u32[]{:S(2)}) collective-permute-start(f32[4,4,64,128]{3,2,1,0:T(8,128)S(1)} %pad_maximum_fusion.1.refs_0_), channel_id=1, source_target_pairs={{6,0},{7,1},{0,2},{1,3},{2,4},{3,5},{4,6},{5,7},{14,8},{15,9},{8,1... | collective-permute-start | bytes 1572872 | tf_op jit(solution)/shard_map/ppermute | solution.py:469
  193.1 49.4 %collective-permute-start.12 = (f32[4,4,64,128]{3,2,1,0:T(8,128)S(1)}, f32[4,4,64,128]{3,2,1,0:T(8,128)S(1)}, u32[]{:S(2)}, u32[]{:S(2)}) collective-permute-start(f32[4,4,64,128]{3,2,1,0:T(8,128)S(1)} %pad_maximum_fusion.1.refs_0_), channel_id=1, source_target_pairs={{0,1},{1,0},{2,3},{3,2},{4,5},{5,4},{6,7},{7,6},{8,9},{9,8},{10,11... | collective-permute-start | bytes 1572872 | tf_op jit(solution)/shard_map/ppermute | solution.py:470
  207.3 35.3 %collective-permute-start.13 = (f32[4,4,64,128]{3,2,1,0:T(8,128)S(1)}, f32[4,4,64,128]{3,2,1,0:T(8,128)S(1)}, u32[]{:S(2)}, u32[]{:S(2)}) collective-permute-start(f32[4,4,64,128]{3,2,1,0:T(8,128)S(1)} %collective-permute-done.9.refs_1_), channel_id=1, source_target_pairs={{0,1},{1,0},{2,3},{3,2},{4,5},{5,4},{6,7},{7,6},{8,9},{9,8},{10,11... | collective-permute-start | bytes 1572872 | tf_op jit(solution)/shard_map/ppermute | solution.py:470
  208.0 34.5 %collective-permute-start.14 = (f32[4,4,64,128]{3,2,1,0:T(8,128)S(1)}, f32[4,4,64,128]{3,2,1,0:T(8,128)}, u32[]{:S(2)}, u32[]{:S(2)}) collective-permute-start(f32[4,4,64,128]{3,2,1,0:T(8,128)S(1)} %collective-permute-done.10.refs_2_), channel_id=1, source_target_pairs={{0,1},{1,0},{2,3},{3,2},{4,5},{5,4},{6,7},{7,6},{8,9},{9,8},{10,11... | collective-permute-start | bytes 1572872 | tf_op jit(solution)/shard_map/ppermute | solution.py:470
  219.2 23.4 %collective-permute-start.15 = (f32[4,4,64,128]{3,2,1,0:T(8,128)S(1)}, f32[4,4,64,128]{3,2,1,0:T(8,128)}, u32[]{:S(2)}, u32[]{:S(2)}) collective-permute-start(f32[4,4,64,128]{3,2,1,0:T(8,128)S(1)} %collective-permute-done.11.refs_3_), channel_id=1, source_target_pairs={{0,1},{1,0},{2,3},{3,2},{4,5},{5,4},{6,7},{7,6},{8,9},{9,8},{10,11... | collective-permute-start | bytes 1572872 | tf_op jit(solution)/shard_map/ppermute | solution.py:470
  220.1 3.7 %copy-start.1 = (f32[8,16,128,128]{3,2,1,0:T(8,128)S(1)}, f32[8,16,128,128]{3,2,1,0:T(8,128)}, u32[]{:S(2)}) copy-start(f32[8,16,128,128]{3,2,1,0:T(8,128)} %param.4) | copy-start | bytes 25165828
  229.5 2.0 copy-start.7
  231.5 3.5 %copy-start.2 = (f32[8,16,128,128]{3,2,1,0:T(8,128)S(1)}, f32[8,16,128,128]{3,2,1,0:T(8,128)}, u32[]{:S(2)}) copy-start(f32[8,16,128,128]{3,2,1,0:T(8,128)} %param.4) | copy-start | bytes 25165828
  290.6 2.0 copy-start.11
  309.2 2.2 copy-start.8
  311.4 2.2 copy-start.10
  (5 other events, 6.8 us)
Sparse Core Ops, SparseCore 0:
  102.9 107.6 all-gather.6
  212.7 70.6 all-gather.4

commit v2 on v1

v2 whole, which is shorter than its diff:
```python
import jax
import jax.numpy as jnp
from jax import lax
from jax.experimental import pallas as pl
from jax.experimental.pallas import tpu as pltpu
from jax.sharding import PartitionSpec as P

B = 128
HB = 64
ROWS = 16
COLS = 8
HALF = 8
LR = 8
LC = 16
CB = 8
PANEL = 1024
f32 = jnp.float32
bf16 = jnp.bfloat16
exact = lax.Precision.HIGHEST
MIB = 2**20
VMEM = 62 * MIB
CHEAP = pl.CostEstimate(flops=2**10, bytes_accessed=2**10, transcendentals=0)


def block_dot(left, right, contract_left=1):
    dims = (((contract_left,), (0,)), ((), ()))
    return lax.dot_general(left, right, dims, preferred_element_type=f32)


def turned_dot(left, right):
    dims = (((1,), (1,)), ((), ()))
    return lax.dot_general(left, right, dims, preferred_element_type=f32)


def exact_dot(left, right, contract_left=1):
    dims = (((contract_left,), (0,)), ((), ()))
    return lax.dot_general(left, right, dims, precision=exact, preferred_element_type=f32)


def split(value):
    high = value.astype(bf16)
    return high, (value - high.astype(f32)).astype(bf16)


def pack_slots(child, table):
    def body(tab, child_ref, out_ref, held, packed, zero, in_sem, out_sem):
        def fetch(i):
            return pltpu.make_async_copy(child_ref.at[i], held.at[i], in_sem.at[i])

        for i in range(CB):
            fetch(i).start()
        zero[...] = jnp.zeros_like(zero)
        for i in range(CB):
            parent = tab[i]
            mine = parent % ROWS
            other = (mine + HALF) % ROWS
            fetch(i).wait()
            for place in range(COLS):
                source = tab[CB + place]
                gain = tab[2 * CB + i * CB + source].astype(f32)
                packed[i, place] = held[i, source] * gain
            pltpu.make_async_copy(packed.at[i], out_ref.at[mine], out_sem.at[i, 0]).start()

            @pl.when(parent < HALF)
            def _():
                pltpu.make_async_copy(packed.at[i], out_ref.at[other], out_sem.at[i, 1]).start()

            @pl.when(parent >= HALF)
            def _():
                pltpu.make_async_copy(zero, out_ref.at[other], out_sem.at[i, 1]).start()

        for i in range(CB):
            for n in range(2):
                pltpu.make_async_copy(zero, out_ref.at[0], out_sem.at[i, n]).wait()

    return pl.pallas_call(
        body,
        in_specs=[
            pl.BlockSpec(memory_space=pltpu.SMEM),
            pl.BlockSpec(memory_space=pl.ANY),
        ],
        out_specs=pl.BlockSpec(memory_space=pl.ANY),
        out_shape=jax.ShapeDtypeStruct((ROWS, COLS, B, B), f32),
        scratch_shapes=[
            pltpu.VMEM((CB, CB, B, B), f32),
            pltpu.VMEM((CB, COLS, B, B), f32),
            pltpu.VMEM((COLS, B, B), f32),
            pltpu.SemaphoreType.DMA((CB,)),
            pltpu.SemaphoreType.DMA((CB, 2)),
        ],
        compiler_params=pltpu.CompilerParams(vmem_limit_bytes=VMEM),
        cost_estimate=CHEAP,
    )(table, child)


def gain_of(code):
    return (code > 0).astype(f32)


def place_of(code):
    return jnp.maximum(code - 1, 0)


NKEYS = LR + 1 + LC


def panel_column(front, arrived, table):
    def body(tab, front_ref, arrived_ref, out_ref, own, got, own_sem, got_sem):
        def fetch(l):
            copies = [pltpu.make_async_copy(front_ref.at[l, 0], own.at[l], own_sem.at[l])]
            for child in range(2):
                base = child * NKEYS
                row = child * HALF + place_of(tab[base + l])
                block = arrived_ref.at[row, place_of(tab[base + LR + 1])]
                copies.append(
                    pltpu.make_async_copy(block, got.at[child, l], got_sem.at[child, l])
                )
            return copies

        for l in range(LR):
            for copy in fetch(l):
                copy.start()
        for l in range(LR):
            for copy in fetch(l):
                copy.wait()
            value = own[l]
            for child in range(2):
                base = child * NKEYS
                value = value + got[child, l] * (
                    gain_of(tab[base + LR + 1]) * gain_of(tab[base + l])
                )
            out_ref[l] = value

    return pl.pallas_call(
        body,
        in_specs=[
            pl.BlockSpec(memory_space=pltpu.SMEM),
            pl.BlockSpec(memory_space=pl.ANY),
            pl.BlockSpec(memory_space=pl.ANY),
        ],
        out_specs=pl.BlockSpec(memory_space=pltpu.VMEM),
        out_shape=jax.ShapeDtypeStruct((LR, B, B), f32),
        scratch_shapes=[
            pltpu.VMEM((LR, B, B), f32),
            pltpu.VMEM((2, LR, B, B), f32),
            pltpu.SemaphoreType.DMA((LR,)),
            pltpu.SemaphoreType.DMA((2, LR)),
        ],
        compiler_params=pltpu.CompilerParams(vmem_limit_bytes=VMEM),
        cost_estimate=CHEAP,
    )(table, front, arrived)


def leading_row(front, received, arrived, table):
    def body(tab, own_ref, recv_ref, first_ref, other_ref, top_ref, lead_ref):
        upper = tab[2 * NKEYS] < HALF
        for m in range(LC):
            value = jnp.where(upper, own_ref[0, m, 0], recv_ref[m])
            for child, ref in ((0, first_ref), (1, other_ref)):
                base = child * NKEYS
                code = tab[base + LR + 1 + m]
                gain = gain_of(code) * gain_of(tab[base + LR])
                value = value + ref[0, place_of(code), 0] * gain
            top_ref[m] = value
        lead_ref[...] = top_ref[0]

    def rows_of(child):
        def pick(step, tab):
            row = child * HALF + place_of(tab[child * NKEYS + LR])
            return row, 0, tab[2 * NKEYS] // HALF, 0, 0

        return pick

    return pl.pallas_call(
        body,
        grid_spec=pltpu.PrefetchScalarGridSpec(
            num_scalar_prefetch=1,
            grid=(1,),
            in_specs=[
                pl.BlockSpec((1, LC, 1, HB, B), lambda step, tab: (0, 0, 0, 0, 0)),
                pl.BlockSpec((LC, HB, B), lambda step, tab: (0, 0, 0)),
                pl.BlockSpec((1, COLS, 1, HB, B), rows_of(0)),
                pl.BlockSpec((1, COLS, 1, HB, B), rows_of(1)),
            ],
            out_specs=[
                pl.BlockSpec((LC, HB, B), lambda step, tab: (0, 0, 0)),
                pl.BlockSpec((HB, B), lambda step, tab: (0, 0)),
            ],
        ),
        out_shape=[
            jax.ShapeDtypeStruct((LC, HB, B), f32),
            jax.ShapeDtypeStruct((HB, B), f32),
        ],
        compiler_params=pltpu.CompilerParams(vmem_limit_bytes=VMEM),
        cost_estimate=CHEAP,
    )(table, front, received, arrived, arrived)


def extend_add(front, arrived, table):
    def body(tab, parent_ref, first_ref, other_ref, out_ref):
        step = pl.program_id(0)
        for m in range(LC):
            value = parent_ref[0, m]
            for child, ref in ((0, first_ref), (1, other_ref)):
                base = child * NKEYS
                code = tab[base + LR + 1 + m]
                gain = gain_of(code) * gain_of(tab[base + step])
                value = value + ref[0, place_of(code)] * gain
            out_ref[0, m] = value

    def rows_of(child):
        return lambda step, tab: (child * HALF + place_of(tab[child * NKEYS + step]), 0, 0, 0)

    return pl.pallas_call(
        body,
        grid_spec=pltpu.PrefetchScalarGridSpec(
            num_scalar_prefetch=1,
            grid=(LR,),
            in_specs=[
                pl.BlockSpec((1, LC, B, B), lambda step, tab: (step, 0, 0, 0)),
                pl.BlockSpec((1, COLS, B, B), rows_of(0)),
                pl.BlockSpec((1, COLS, B, B), rows_of(1)),
            ],
            out_specs=pl.BlockSpec((1, LC, B, B), lambda step, tab: (step, 0, 0, 0)),
        ),
        out_shape=jax.ShapeDtypeStruct((LR, LC, B, B), f32),
        compiler_params=pltpu.CompilerParams(vmem_limit_bytes=VMEM),
        cost_estimate=CHEAP,
    )(table, front, arrived, arrived)


def factor_block(block):
    lane = lax.broadcasted_iota(jnp.int32, (8, B), 1)
    sub = lax.broadcasted_iota(jnp.int32, (8, B), 0)

    def lanes(tile, j):
        return jnp.broadcast_to(tile[:, j : j + 1], (8, B))

    def subs(tile, k):
        return jnp.broadcast_to(tile[k : k + 1, :], (8, B))

    tiles = [block[8 * r : 8 * r + 8, :] for r in range(B // 8)]
    for group in range(B // 8):
        low = 8 * group
        own = [lanes(tiles[group], low + k) for k in range(8)]
        work = tiles[group]
        inside = jnp.logical_and(lane >= low, lane < low + 8)
        upper = []
        for k in range(0, 8, 2):
            n = k + 1
            a, b, c = subs(own[k], k), subs(own[n], k), subs(own[n], n)
            det = 1.0 / (a * c - b * b)
            at_k, at_n = lane == low + k, lane == low + n
            on_k, on_n = sub == k, sub == n
            on = jnp.logical_or(on_k, on_n)
            row_k, row_n = subs(work, k), subs(work, n)
            upper.append(row_k)
            ratio = b * (1.0 / a)
            upper.append(jnp.where(at_k, 0.0, row_n) - ratio * jnp.where(at_k, 1.0, row_k))
            row_k = jnp.where(at_k, 1.0, jnp.where(at_n, 0.0, row_k))
            row_n = jnp.where(at_n, 1.0, jnp.where(at_k, 0.0, row_n))
            new_k = det * (c * row_k - b * row_n)
            new_n = det * (a * row_n - b * row_k)
            coef_k = jnp.where(on_k, -1.0, jnp.where(on_n, 0.0, own[k]))
            coef_n = jnp.where(on_n, -1.0, jnp.where(on_k, 0.0, own[n]))
            clear = jnp.logical_or(jnp.logical_or(at_k, at_n), on)
            work = jnp.where(clear, 0.0, work) - coef_k * new_k - coef_n * new_n
            for m in range(k + 2, 8):
                x, y = subs(own[m], k), subs(own[m], n)
                step = coef_k * (det * (c * x - b * y)) + coef_n * (det * (a * y - b * x))
                own[m] = jnp.where(on, 0.0, own[m]) - step
        solved = [subs(work, k) for k in range(8)]
        rows = upper[0]
        for k in range(1, 8):
            rows = jnp.where(sub == k, upper[k], rows)
        tiles[group] = rows
        for r in range(group + 1, B // 8):
            value = jnp.where(inside, 0.0, tiles[r])
            for k in range(8):
                value = value - lanes(tiles[r], low + k) * solved[k]
            tiles[r] = value
    return jnp.concatenate(tiles, axis=0)


def leading_factor(pieces, where):
    def body(at, *refs):
        piece_refs, (w, diag) = refs[:10], refs[10:]
        for n, ref in enumerate(piece_refs):
            dk, dy = n // 5, (0, 1, 3, 2, 2)[n % 5]
            q = ((at[2] + dy) % 4) * 2 + (at[3] + dk) % 2
            for dx in range(ref.shape[0]):
                x = (at[0] + dx + (2 if n % 5 == 4 else 0)) % 4
                for dz in range(4):
                    g = (x % 2) * 4 + (at[1] + dz) % 4
                    top = pl.multiple_of(g * B + (x // 2) * HB, HB)
                    w[pl.ds(top, HB), pl.ds(pl.multiple_of(q * B, B), B)] = ref[dx, dz]
        row = lax.broadcasted_iota(jnp.int32, (B, B), 0)
        col = lax.broadcasted_iota(jnp.int32, (B, B), 1)

        def step(kb, carry):
            o = pl.multiple_of(kb * B, B)
            f = factor_block(w[pl.ds(o, B), pl.ds(o, B)])
            pivots = jnp.sum(jnp.where(row == col, f, 0.0), axis=1, keepdims=True)
            scale = 1.0 / jnp.sqrt(pivots)
            inverse = jnp.where(row > col, f, (row == col).astype(f32)) * scale
            diag[pl.ds(o, B), :] = jnp.where(row <= col, f, 0.0) * scale
            w[pl.ds(o, B), :] = exact_dot(inverse, w[pl.ds(o, B), :])
            w[pl.ds(o, B), pl.ds(o, B)] = inverse

            @pl.when(kb % 2 == 0)
            def _():
                n = pl.multiple_of(o + B, B)
                w[pl.ds(n, B), pl.ds(o, B)] = jnp.zeros((B, B), f32)
                w[pl.ds(n, B), :] -= exact_dot(w[pl.ds(o, B), pl.ds(n, B)], w[pl.ds(o, B), :], 0)

            for done in range(256, PANEL, 256):

                @pl.when(kb == done // B - 1)
                def _():
                    above = (slice(done - 256, done - B), slice(done - B, done))
                    kept = w[above]
                    w[above] = jnp.zeros((B, B), f32)
                    w[done:, done - 256 : done] = jnp.zeros((PANEL - done, 256), f32)
                    for n in range(done, PANEL, 256):
                        left = w[done - 256 : done, n : n + 256]
                        w[n : n + 256, :] -= exact_dot(left, w[done - 256 : done, :], 0)
                    w[above] = kept

            return carry

        lax.fori_loop(0, PANEL // B, step, 0)

    return pl.pallas_call(
        body,
        in_specs=[pl.BlockSpec(memory_space=pltpu.SMEM)]
        + [pl.BlockSpec(memory_space=pltpu.VMEM)] * 10,
        out_specs=[pl.BlockSpec(memory_space=pltpu.VMEM)] * 2,
        out_shape=[
            jax.ShapeDtypeStruct((PANEL, PANEL), f32),
            jax.ShapeDtypeStruct((PANEL, B), f32),
        ],
        compiler_params=pltpu.CompilerParams(vmem_limit_bytes=VMEM),
        cost_estimate=CHEAP,
    )(where, *pieces)


def panel_solve(rows, w, diag, where):
    def body(at, rows_ref, w_ref, diag_ref, high_ref, low_ref, out_ref, rh, rl, wh, wl, below, bh, bl):
        p, q = at[0], at[1]
        for e in range(COLS):
            for l in range(LR):
                high, low = split(rows_ref[e, l])
                rh[l * B : (l + 1) * B, e * B : (e + 1) * B] = high
                rl[l * B : (l + 1) * B, e * B : (e + 1) * B] = low
        for r in range(0, PANEL, 256):
            shape = (256, r + 256)
            under = (
                lax.broadcasted_iota(jnp.int32, shape, 0) + r
                >= lax.broadcasted_iota(jnp.int32, shape, 1)
            )
            high, low = split(jnp.where(under, w_ref[r : r + 256, : r + 256], 0.0))
            wh[r : r + 256, : r + 256] = high
            wl[r : r + 256, : r + 256] = low
            value = turned_dot(rh[:, : r + 256], high)
            value += turned_dot(rl[:, : r + 256], high)
            value += turned_dot(rh[:, : r + 256], low)
            below[:, r : r + 256] = value
            high, low = split(value)
            bh[:, r : r + 256] = high
            bl[:, r : r + 256] = low
        mine = pl.ds(pl.multiple_of(q * B, B), B)
        for l in range(LR):
            out_ref[l] = below[l * B : (l + 1) * B, mine]

        @pl.when(p < HALF)
        def _():
            over = w_ref[mine, pl.ds(pl.multiple_of((p % HALF) * B, B), B)]
            top = jnp.where(p > q, over, jnp.where(p == q, diag_ref[mine, :], 0.0))
            out_ref[0] = top.T

        for r in range(0, PANEL, 256):
            value = block_dot(bh[:, r:], wh[r:, r : r + 256])
            value += block_dot(bl[:, r:], wh[r:, r : r + 256])
            value += block_dot(bh[:, r:], wl[r:, r : r + 256])
            high, low = split(value)
            high_ref[:, r : r + 256] = high
            low_ref[:, r : r + 256] = low

        @pl.when(p < HALF)
        def _():
            high_ref[:B, :] = jnp.zeros((B, PANEL), bf16)
            low_ref[:B, :] = jnp.zeros((B, PANEL), bf16)

    return pl.pallas_call(
        body,
        in_specs=[pl.BlockSpec(memory_space=pltpu.SMEM)]
        + [pl.BlockSpec(memory_space=pltpu.VMEM)] * 3,
        out_specs=[pl.BlockSpec(memory_space=pltpu.VMEM)] * 3,
        out_shape=[
            jax.ShapeDtypeStruct((PANEL, PANEL), bf16),
            jax.ShapeDtypeStruct((PANEL, PANEL), bf16),
            jax.ShapeDtypeStruct((LR, B, B), f32),
        ],
        scratch_shapes=[
            pltpu.VMEM((PANEL, PANEL), bf16),
            pltpu.VMEM((PANEL, PANEL), bf16),
            pltpu.VMEM((PANEL, PANEL), bf16),
            pltpu.VMEM((PANEL, PANEL), bf16),
            pltpu.VMEM((PANEL, PANEL), f32),
            pltpu.VMEM((PANEL, PANEL), bf16),
            pltpu.VMEM((PANEL, PANEL), bf16),
        ],
        compiler_params=pltpu.CompilerParams(vmem_limit_bytes=VMEM),
        cost_estimate=CHEAP,
    )(where, rows, w, diag)


def trailing_update(assembled, columns, high, low, panel):
    def body(front_ref, col_ref, high_ref, low_ref, panel_ref, out_ref, ch, cl):
        for p in range(ROWS):
            top = (p % HALF) * B + (p // HALF) * HB
            for n in range(2):
                hi, lo = split(col_ref[p, n])
                ch[top : top + HB, n * B : (n + 1) * B] = hi
                cl[top : top + HB, n * B : (n + 1) * B] = lo
        for r in range(0, PANEL, 256):
            value = block_dot(high_ref[r : r + 256, :], ch[...])
            value += block_dot(high_ref[r : r + 256, :], cl[...])
            value += block_dot(low_ref[r : r + 256, :], ch[...])
            for l in range(r // B, r // B + 2):
                for n in range(2):
                    s = l * B - r
                    out_ref[l, n] = front_ref[l, n] - value[s : s + B, n * B : (n + 1) * B]

        @pl.when(pl.program_id(0) == 0)
        def _():
            for l in range(LR):
                out_ref[l, 0] = panel_ref[l]

    blocks = pl.BlockSpec((LR, 2, B, B), lambda step: (0, step, 0, 0))
    whole = pl.BlockSpec((PANEL, PANEL), lambda step: (0, 0))
    return pl.pallas_call(
        body,
        grid=(LC // 2,),
        in_specs=[
            blocks,
            pl.BlockSpec((ROWS, 2, HB, B), lambda step: (0, step, 0, 0)),
            whole,
            whole,
            pl.BlockSpec((LR, B, B), lambda step: (0, 0, 0)),
        ],
        out_specs=blocks,
        out_shape=jax.ShapeDtypeStruct((LR, LC, B, B), f32),
        scratch_shapes=[pltpu.VMEM((PANEL, 256), bf16), pltpu.VMEM((PANEL, 256), bf16)],
        compiler_params=pltpu.CompilerParams(vmem_limit_bytes=VMEM),
        cost_estimate=CHEAP,
    )(assembled, columns, high, low, panel)


def along_x(distance):
    return [(4 * ((x + distance) % 4) + z, 4 * x + z) for x in range(4) for z in range(4)]


def along_z(distance):
    return [(4 * x + (z + distance) % 4, 4 * x + z) for x in range(4) for z in range(4)]


def along_y(distance):
    return [(2 * ((y + distance) % 4) + k, 2 * y + k) for y in range(4) for k in range(2)]


OTHER_CORE = [(q, q ^ 1) for q in range(COLS)]


def shards(parent_front, child_updates, child_mask, child_map):
    p = lax.axis_index("row")
    q = lax.axis_index("col")
    both = ("row", "col")
    front = parent_front.reshape(LR, LC, 2, HB, B)

    own_map = child_map[p // HALF].reshape(CB, CB)
    row_parent = own_map[:, p % HALF]
    col_parent = own_map[:, q]
    index = jnp.arange(CB)
    column = jnp.sum((col_parent[None] % COLS == index[:, None]) * index[None], axis=1)
    source_table = jnp.concatenate([row_parent, column, child_mask.reshape(-1)]).astype(jnp.int32)

    keys = jnp.concatenate(
        [jnp.arange(LR) * ROWS + p, (p % HALF)[None], jnp.arange(LC) * COLS + q]
    )
    hits = child_map[:, None, :] == keys[None, :, None]
    codes = jnp.sum(hits * (jnp.arange(CB * CB) % CB + 1)[None, None], axis=2)
    target_table = jnp.concatenate([codes.reshape(-1), p[None]]).astype(jnp.int32)

    top_other = lax.ppermute(front[0, :, 1], "row", [(i, i + HALF) for i in range(HALF)])

    slots = pack_slots(child_updates, source_table)
    arrived = lax.all_to_all(
        slots.reshape(ROWS * COLS, B, B), both, 0, 0, tiled=True
    ).reshape(ROWS, COLS, B, B)

    target_table, top_other = lax.optimization_barrier((target_table, top_other))
    column = panel_column(parent_front, arrived, target_table)
    panel_rows = lax.all_gather(column, "col", axis=0)

    halves = arrived.reshape(ROWS, COLS, 2, HB, B)
    top, lead = leading_row(front, top_other, halves, target_table)
    columns = lax.all_gather(top, "row", axis=0)

    near = [lead] + [lax.ppermute(lead, "row", along_z(d)) for d in range(1, 4)]
    stacked = jnp.stack(near)
    near = [stacked] + [lax.ppermute(stacked, "row", along_x(d)) for d in range(1, 4)]
    stacked = jnp.stack(near)
    ahead = lax.ppermute(stacked, "col", along_y(1))
    back = lax.ppermute(stacked, "col", along_y(3))
    assembled = extend_add(parent_front, arrived, target_table)
    assembled, ahead, back = lax.optimization_barrier((assembled, ahead, back))
    far = [
        lax.ppermute(ahead[:2], "col", along_y(1)),
        lax.ppermute(back[2:], "col", along_y(3)),
    ]
    near = [stacked, ahead, back] + far
    near = near + [lax.ppermute(piece, "col", OTHER_CORE) for piece in near]

    where = jnp.stack([p // 4, p % 4, q // 2, q % 2]).astype(jnp.int32)
    w, diag = leading_factor(near, where)
    high, low, panel = panel_solve(panel_rows, w, diag, jnp.stack([p, q]).astype(jnp.int32))
    return trailing_update(assembled, columns, high, low, panel)


def solution(mesh):
    in_specs = (P("row", "col", None, None), P("row", "col", None, None), P("row", "col"), P())
    out_specs = P("row", "col", None, None)
    return jax.shard_map(shards, mesh=mesh, in_specs=in_specs, out_specs=out_specs, check_vma=False)
```

time: 341 us -> 291 us (0.85)
  local copies, waits for them, and re-layouts: 37.1 us -> 4.56 us
  starting transfers between devices: 73.4 us -> 45.9 us
  Pallas kernels: 96.6 us -> 107 us
    ppermute x1, waiting for transfers between devices: 47.5 us -> 94.4 us  [shards(): lax.ppermute(front[0, :, 1], 'row', [(i, i + HALF) for i in range(HALF)])]
    unnamed x34 -> x18, local copies, waits for them, and re-layouts: 34.1 us -> 1.5 us
    all_to_all x2 -> x1, starting transfers between devices: 39.2 us -> 12 us  [shards(): lax.all_to_all(slots.reshape(ROWS * COLS, B, B), both, 0, 0, tiled=True)]
    ppermute x5 -> x4, waiting for transfers between devices: 28.4 us -> 5.51 us  [the longest x1 2.3 us: shards(): ahead = lax.ppermute(stacked, 'col', along_y(1))]
    ppermute x3, waiting for transfers between devices: 25.7 us -> 6.16 us  [shards(): lax.ppermute(stacked, 'row', along_x(d))]
    ppermute x3, waiting for transfers between devices: 14.8 us -> 3.43 us  [shards(): near = [lead] + [lax.ppermute(lead, 'row', along_z(d)) for d in range(1, 4)]]
    ppermute x5 -> x4, starting transfers between devices: 12.3 us -> 3.13 us  [the longest x1 1.45 us: shards(): back = lax.ppermute(stacked, 'col', along_y(3))]
    ppermute x4 -> x5, starting transfers between devices: 4.5 us -> 10.7 us  [shards(): near = near + [lax.ppermute(piece, 'col', OTHER_CORE) for piece in near]]
  transfers between devices with their start and end apart: 20 -> 19, of which waited for: 11 -> 12; matrix products, arithmetic and copies ran while one was open for 1% -> 2% of each run, Pallas kernels for 22% -> 28%
where the time goes in v2:
time: 291 us; the launch traced here: 290 us
  waiting for transfers between devices  114 us (39%)
  Pallas kernels  107 us (37%)
  starting transfers between devices  45.9 us (16%)
  between operations  13.6 us (5%)
  local copies, waits for them, and re-layouts  4.56 us (2%)
  other arithmetic  4.01 us (1%)
    ppermute x1, waiting for transfers between devices, shards(): lax.ppermute(front[0, :, 1], 'row', [(i, i + HALF) for i in range(HALF)])  94.4 us
    pallas_call x1, Pallas kernels, leading_factor(): pl.pallas_call(body, in_specs=[pl.BlockSpec(memory_space=pltpu.SMEM)] + [...  50 us
    pallas_call x1, Pallas kernels, trailing_update(): pl.pallas_call(body, grid=(LC // 2,), in_specs=[blocks, pl.BlockSpec((ROW...  19 us
    pallas_call x1, Pallas kernels, panel_solve(): pl.pallas_call(body, in_specs=[pl.BlockSpec(memory_space=pltpu.SMEM)] + [...  16.1 us
    all_to_all x1, starting transfers between devices, shards(): lax.all_to_all(slots.reshape(ROWS * COLS, B, B), both, 0, 0, tiled=True)  12 us
    ppermute x3, starting transfers between devices, shards(): lax.ppermute(stacked, 'row', along_x(d))  11.4 us
    pallas_call x1, Pallas kernels, extend_add(): pl.pallas_call(body, grid_spec=pltpu.PrefetchScalarGridSpec(num_scalar_pr...  10.8 us
    ppermute x5, starting transfers between devices, shards(): near = near + [lax.ppermute(piece, 'col', OTHER_CORE) for piece in near]  10.7 us
  transfers between devices with their start and end apart: 19, of which 12 were waited for; matrix products, arithmetic and copies ran while one was open for 2% of the time, Pallas kernels for 28%

profile of v2, /device:TPU:1, one launch (start us, length us, event | category | flops | bytes accessed | tf_op | source)
XLA Modules:
  0.0 289.6 jit_solution(7388523059997157710)
XLA Ops:
  7.7 0.8 reshape.57
  9.0 5.2 %shard_map.46 = f32[16,8,128,128]{3,2,1,0:T(8,128)} custom-call(s32[80]{0:T(128)} %pad_add_fusion.2.tab, f32[8,8,128,128]{3,2,1,0:T(8,128)} %child_ref.1), custom_call_target="tpu_custom_call" | custom-call | flops 1024 | bytes 1024 | tf_op jit(solution)/shard_map/pallas_call | solution.py:76
  14.3 12.0 %all-to-all-start = ((f32[128,128,128]{2,1,0:T(8,128)}), f32[128,128,128]{2,1,0:T(8,128)}, u32[]{:S(2)}, u32[]{:S(2)}) async-start(f32[128,128,128]{2,1,0:T(8,128)} %bitcast.28), calls=%async_computation | async-start | bytes 16777216 | tf_op jit(solution)/shard_map/all_to_all | solution.py:498
  26.3 1.1 slice_bitcast_fusion
  27.4 4.8 %collective-permute-start = (f32[16,64,128]{2,1,0:T(8,128)S(1)}, f32[16,64,128]{2,1,0:T(8,128)S(1)}, u32[]{:S(2)}, u32[]{:S(2)}) collective-permute-start(f32[16,64,128]{2,1,0:T(8,128)S(1)} %slice_bitcast_fusion), channel_id=1, source_target_pairs={{0,64},{8,72},{16,80},{24,88},{32,96},{40,104},{48,112},{56,120},{... | collective-permute-start | bytes 1572872 | tf_op jit(solution)/shard_map/ppermute | solution.py:495
  33.7 94.4 %collective-permute-done.recv_ref = f32[16,64,128]{2,1,0:T(8,128)S(1)} collective-permute-done((f32[16,64,128]{2,1,0:T(8,128)S(1)}, f32[16,64,128]{2,1,0:T(8,128)S(1)}, u32[]{:S(2)}, u32[]{:S(2)}) %collective-permute-start) | collective-permute-done | bytes 524320 | tf_op jit(solution)/shard_map/ppermute | solution.py:495
  128.2 4.5 %all-to-all-done = f32[128,128,128]{2,1,0:T(8,128)} async-done(((f32[128,128,128]{2,1,0:T(8,128)}), f32[128,128,128]{2,1,0:T(8,128)}, u32[]{:S(2)}, u32[]{:S(2)}) %all-to-all-start) | async-done | bytes 8388640 | tf_op jit(solution)/shard_map/all_to_all | solution.py:498
  132.7 3.3 %shard_map.49 = f32[8,128,128]{2,1,0:T(8,128)} custom-call(s32[51]{0:T(128)} %pad_add_fusion.1.tab, f32[8,16,128,128]{3,2,1,0:T(8,128)} %front_ref.1, f32[16,8,128,128]{3,2,1,0:T(8,128)} %bitcast.5.first_ref.other_ref.arrived_ref), custom_call_target="tpu_custom_call" | custom-call | flops 1024 | bytes 1024 | tf_op jit(solution)/shard_map/pallas_call | solution.py:134
  136.1 3.0 %shard_map.48 = (f32[16,64,128]{2,1,0:T(8,128)}, f32[64,128]{1,0:T(8,128)}) custom-call(s32[51]{0:T(128)} %pad_add_fusion.1.tab, f32[8,16,2,64,128]{4,3,2,1,0:T(8,128)} %bitcast.27, f32[16,64,128]{2,1,0:T(8,128)} %copy-done.5, f32[16,8,2,64,128]{4,3,2,1,0:T(8,128)} %bitcast.6.first_ref.other_ref, f32[16,8,2,64,128]{4,3,2,1,0:T(8,128)} %bitcast.6.first_ref.other_ref), custom_call_target="tpu_custom_call" | custom-call | flops 1024 | bytes 1024 | tf_op jit(solution)/shard_map/pallas_call | solution.py:174
  139.1 1.7 collective-permute-start.3
  140.8 1.1 collective-permute-start.1
  141.8 1.1 collective-permute-start.2
  143.7 2.6 collective-permute-done.2
  146.3 0.8 fusion.4
  147.1 10.7 %collective-permute-start.4 = (f32[4,64,128]{2,1,0:T(8,128)S(1)}, f32[4,64,128]{2,1,0:T(8,128)S(1)}, u32[]{:S(2)}, u32[]{:S(2)}) collective-permute-start(f32[4,64,128]{2,1,0:T(8,128)S(1)} %get-tuple-element.32), channel_id=1, source_target_pairs={{32,0},{40,8},{48,16},{56,24},{64,32},{72,40},{80,48},{88,56},{96,... | collective-permute-start | bytes 393224 | tf_op jit(solution)/shard_map/ppermute | solution.py:512
  158.5 2.6 collective-permute-done.4
  161.1 2.1 collective-permute-done.5
  163.2 1.4 collective-permute-done.6
  164.8 1.5 collective-permute-start.8
  166.2 10.8 %shard_map.47.front_ref = f32[8,16,128,128]{3,2,1,0:T(8,128)} custom-call(s32[51]{0:T(128)} %pad_add_fusion.1.tab, f32[8,16,128,128]{3,2,1,0:T(8,128)} %front_ref.1, f32[16,8,128,128]{3,2,1,0:T(8,128)} %bitcast.5.first_ref.other_ref.arrived_ref, f32[16,8,128,128]{3,2,1,0:T(8,128)} %bitcast.5.first_ref.other_ref.arrived_ref), custom_call_target="tpu_custom_call" | custom-call | flops 1024 | bytes 1024 | tf_op jit(solution)/shard_map/pallas_call | solution.py:214
  177.0 4.0 %collective-permute-start.11 = (f32[4,4,64,128]{3,2,1,0:T(8,128)S(1)}, f32[4,4,64,128]{3,2,1,0:T(8,128)S(1)}, u32[]{:S(2)}, u32[]{:S(2)}) collective-permute-start(f32[4,4,64,128]{3,2,1,0:T(8,128)S(1)} %pad_maximum_fusion.refs_0_), channel_id=1, source_target_pairs={{0,1},{1,0},{2,3},{3,2},{4,5},{5,4},{6,7},{7,6},{8,9},{9,8},{10,11... | collective-permute-start | bytes 1572872 | tf_op jit(solution)/shard_map/ppermute | solution.py:523
  181.0 2.3 collective-permute-done.7.refs_1_
  183.3 1.0 collective-permute-done.8.refs_2_
  184.9 1.1 collective-permute-start.10
  185.9 2.3 collective-permute-start.12
  188.2 2.2 collective-permute-done.9.refs_3_
  190.5 2.6 collective-permute-start.14
  193.1 1.8 collective-permute-start.15
  196.9 0.8 copy-done.4
  197.7 50.0 %shard_map.50 = (f32[1024,1024]{1,0:T(8,128)}, f32[1024,128]{1,0:T(8,128)}) custom-call(s32[4]{0:T(128)} %pad_add_fusion.4.at, f32[4,4,64,128]{3,2,1,0:T(8,128)} %copy-done, f32[4,4,64,128]{3,2,1,0:T(8,128)} %copy-done.1, f32[4,4,64,128]{3,2,1,0:T(8,128)} %copy-done.2, f32[2,4,64,128]{3,2,1,0:T(8,128)} %copy-done.6, f32[2,4,64,128]{3,2,1,0:T(8,128)} %copy-done.7, ...), custom_call_target="tpu_custom_call" | custom-call | flops 1024 | bytes 1024 | tf_op jit(solution)/shard_map/pallas_call | solution.py:333
  247.6 16.1 %shard_map.51 = (bf16[1024,1024]{1,0:T(8,128)(2,1)}, bf16[1024,1024]{1,0:T(8,128)(2,1)}, f32[8,128,128]{2,1,0:T(8,128)}) custom-call(s32[2]{0:T(128)} %pad_add_fusion.3.at, f32[8,8,128,128]{3,2,1,0:T(8,128)} %bitcast.30, f32[1024,1024]{1,0:T(8,128)} %get-tuple-element.24.w_ref, f32[1024,128]{1,0:T(8,128)} %get-tuple-element.25.diag_ref), custom_call_target="tpu_custom_call" | custom-call | flops 1024 | bytes 1024 | tf_op jit(solution)/shard_map/pallas_call | solution.py:394
  263.7 19.0 %shard_map.52 = f32[8,16,128,128]{3,2,1,0:T(8,128)} custom-call(f32[8,16,128,128]{3,2,1,0:T(8,128)} %shard_map.47.front_ref, f32[16,16,64,128]{3,2,1,0:T(8,128)} %bitcast.29, bf16[1024,1024]{1,0:T(8,128)(2,1)} %get-tuple-element.26.high_ref, bf16[1024,1024]{1,0:T(8,128)(2,1)} %get-tuple-element.27.low_ref, f32[8,128,128]{2,1,0:T(8,128)} %get-tuple-element.28.panel_ref), custom_call_target="tpu_custom_call" | custom-call | flops 1024 | bytes 1024 | tf_op jit(solution)/shard_map/pallas_call | solution.py:442
  (55 shorter events, 7.5 us)
Async XLA Ops:
  14.3 18.1 %copy-start.8 = (s32[2,64]{1,0:T(2,128)S(1)}, s32[2,64]{1,0:T(2,128)}, u32[]{:S(2)}) copy-start(s32[2,64]{1,0:T(2,128)} %param.7) | copy-start | bytes 1540
  14.3 118.4 %all-to-all-start = ((f32[128,128,128]{2,1,0:T(8,128)}), f32[128,128,128]{2,1,0:T(8,128)}, u32[]{:S(2)}, u32[]{:S(2)}) async-start(f32[128,128,128]{2,1,0:T(8,128)} %bitcast.28), calls=%async_computation | async-start | bytes 16777216 | tf_op jit(solution)/shard_map/all_to_all | solution.py:498
  26.3 221.4 %all-gather.7.cloned.1.call-start = ((), (), s32[]{:S(2)}) async-start(), calls=%async_computation.2 | async-start | bytes 4718592 | tf_op jit(solution)/shard_map/all_gather | solution.py:504
  27.4 100.8 %collective-permute-start = (f32[16,64,128]{2,1,0:T(8,128)S(1)}, f32[16,64,128]{2,1,0:T(8,128)S(1)}, u32[]{:S(2)}, u32[]{:S(2)}) collective-permute-start(f32[16,64,128]{2,1,0:T(8,128)S(1)} %slice_bitcast_fusion), channel_id=1, source_target_pairs={{0,64},{8,72},{16,80},{24,88},{32,96},{40,104},{48,112},{56,120},{... | collective-permute-start | bytes 1572872 | tf_op jit(solution)/shard_map/ppermute | solution.py:495
  128.2 7.8 %copy-start.5 = (f32[16,64,128]{2,1,0:T(8,128)}, f32[16,64,128]{2,1,0:T(8,128)S(1)}, u32[]{:S(2)}) copy-start(f32[16,64,128]{2,1,0:T(8,128)S(1)} %collective-permute-done.recv_ref) | copy-start | bytes 1572868
  136.0 127.7 %all-gather.5.cloned.1.call-start = ((), (), s32[]{:S(2)}) async-start(), calls=%async_computation.1 | async-start | bytes 8912896 | tf_op jit(solution)/shard_map/all_gather | solution.py:508
  139.1 4.3 %collective-permute-start.3 = (f32[64,128]{1,0:T(8,128)}, f32[64,128]{1,0:T(8,128)S(1)}, u32[]{:S(2)}, u32[]{:S(2)}) collective-permute-start(f32[64,128]{1,0:T(8,128)} %get-tuple-element.19), channel_id=1, source_target_pairs={{24,0},{0,8},{8,16},{16,24},{56,32},{32,40},{40,48},{48,56},{88,64... | collective-permute-start | bytes 98312 | tf_op jit(solution)/shard_map/ppermute | solution.py:510
  140.8 3.0 %collective-permute-start.1 = (f32[64,128]{1,0:T(8,128)}, f32[64,128]{1,0:T(8,128)S(1)}, u32[]{:S(2)}, u32[]{:S(2)}) collective-permute-start(f32[64,128]{1,0:T(8,128)} %get-tuple-element.19), channel_id=1, source_target_pairs={{8,0},{16,8},{24,16},{0,24},{40,32},{48,40},{56,48},{32,56},{72,64... | collective-permute-start | bytes 98312 | tf_op jit(solution)/shard_map/ppermute | solution.py:510
  141.8 4.5 %collective-permute-start.2 = (f32[64,128]{1,0:T(8,128)}, f32[64,128]{1,0:T(8,128)S(1)}, u32[]{:S(2)}, u32[]{:S(2)}) collective-permute-start(f32[64,128]{1,0:T(8,128)} %get-tuple-element.19), channel_id=1, source_target_pairs={{16,0},{24,8},{0,16},{8,24},{48,32},{56,40},{32,48},{40,56},{80,64... | collective-permute-start | bytes 98312 | tf_op jit(solution)/shard_map/ppermute | solution.py:510
  147.1 14.0 %collective-permute-start.4 = (f32[4,64,128]{2,1,0:T(8,128)S(1)}, f32[4,64,128]{2,1,0:T(8,128)S(1)}, u32[]{:S(2)}, u32[]{:S(2)}) collective-permute-start(f32[4,64,128]{2,1,0:T(8,128)S(1)} %get-tuple-element.32), channel_id=1, source_target_pairs={{32,0},{40,8},{48,16},{56,24},{64,32},{72,40},{80,48},{88,56},{96,... | collective-permute-start | bytes 393224 | tf_op jit(solution)/shard_map/ppermute | solution.py:512
  157.8 5.4 %collective-permute-start.5 = (f32[4,64,128]{2,1,0:T(8,128)S(1)}, f32[4,64,128]{2,1,0:T(8,128)S(1)}, u32[]{:S(2)}, u32[]{:S(2)}) collective-permute-start(f32[4,64,128]{2,1,0:T(8,128)S(1)} %get-tuple-element.32), channel_id=1, source_target_pairs={{64,0},{72,8},{80,16},{88,24},{96,32},{104,40},{112,48},{120,56},{... | collective-permute-start | bytes 393224 | tf_op jit(solution)/shard_map/ppermute | solution.py:512
  157.8 6.8 %collective-permute-start.6 = (f32[4,64,128]{2,1,0:T(8,128)S(1)}, f32[4,64,128]{2,1,0:T(8,128)S(1)}, u32[]{:S(2)}, u32[]{:S(2)}) collective-permute-start(f32[4,64,128]{2,1,0:T(8,128)S(1)} %get-tuple-element.32), channel_id=1, source_target_pairs={{96,0},{104,8},{112,16},{120,24},{0,32},{8,40},{16,48},{24,56},{32... | collective-permute-start | bytes 393224 | tf_op jit(solution)/shard_map/ppermute | solution.py:512
  164.7 12.3 %copy-start = (f32[4,4,64,128]{3,2,1,0:T(8,128)}, f32[4,4,64,128]{3,2,1,0:T(8,128)S(1)}, u32[]{:S(2)}) copy-start(f32[4,4,64,128]{3,2,1,0:T(8,128)S(1)} %pad_maximum_fusion.refs_0_) | copy-start | bytes 1572868
  164.7 18.6 %collective-permute-start.7 = (f32[4,4,64,128]{3,2,1,0:T(8,128)S(1)}, f32[4,4,64,128]{3,2,1,0:T(8,128)S(1)}, u32[]{:S(2)}, u32[]{:S(2)}) collective-permute-start(f32[4,4,64,128]{3,2,1,0:T(8,128)S(1)} %pad_maximum_fusion.refs_0_), channel_id=1, source_target_pairs={{2,0},{3,1},{4,2},{5,3},{6,4},{7,5},{0,6},{1,7},{10,8},{11,9},{12,... | collective-permute-start | bytes 1572872 | tf_op jit(solution)/shard_map/ppermute | solution.py:514
  164.8 19.5 %collective-permute-start.8 = (f32[4,4,64,128]{3,2,1,0:T(8,128)S(1)}, f32[4,4,64,128]{3,2,1,0:T(8,128)S(1)}, u32[]{:S(2)}, u32[]{:S(2)}) collective-permute-start(f32[4,4,64,128]{3,2,1,0:T(8,128)S(1)} %pad_maximum_fusion.refs_0_), channel_id=1, source_target_pairs={{6,0},{7,1},{0,2},{1,3},{2,4},{3,5},{4,6},{5,7},{14,8},{15,9},{8,1... | collective-permute-start | bytes 1572872 | tf_op jit(solution)/shard_map/ppermute | solution.py:515
  177.0 19.1 %collective-permute-start.11 = (f32[4,4,64,128]{3,2,1,0:T(8,128)S(1)}, f32[4,4,64,128]{3,2,1,0:T(8,128)S(1)}, u32[]{:S(2)}, u32[]{:S(2)}) collective-permute-start(f32[4,4,64,128]{3,2,1,0:T(8,128)S(1)} %pad_maximum_fusion.refs_0_), channel_id=1, source_target_pairs={{0,1},{1,0},{2,3},{3,2},{4,5},{5,4},{6,7},{7,6},{8,9},{9,8},{10,11... | collective-permute-start | bytes 1572872 | tf_op jit(solution)/shard_map/ppermute | solution.py:523
  183.3 14.3 %copy-start.1 = (f32[4,4,64,128]{3,2,1,0:T(8,128)}, f32[4,4,64,128]{3,2,1,0:T(8,128)S(1)}, u32[]{:S(2)}) copy-start(f32[4,4,64,128]{3,2,1,0:T(8,128)S(1)} %collective-permute-done.7.refs_1_) | copy-start | bytes 1572868
  184.3 13.4 %copy-start.2 = (f32[4,4,64,128]{3,2,1,0:T(8,128)}, f32[4,4,64,128]{3,2,1,0:T(8,128)S(1)}, u32[]{:S(2)}) copy-start(f32[4,4,64,128]{3,2,1,0:T(8,128)S(1)} %collective-permute-done.8.refs_2_) | copy-start | bytes 1572868
  184.3 6.2 %collective-permute-start.9 = (f32[2,4,64,128]{3,2,1,0:T(8,128)S(1)}, f32[2,4,64,128]{3,2,1,0:T(8,128)S(1)}, u32[]{:S(2)}, u32[]{:S(2)}) collective-permute-start(f32[2,4,64,128]{3,2,1,0:T(8,128)S(1)} %slice.10), channel_id=1, source_target_pairs={{2,0},{3,1},{4,2},{5,3},{6,4},{7,5},{0,6},{1,7},{10,8},{11,9},{12,... | collective-permute-start | bytes 786440 | tf_op jit(solution)/shard_map/ppermute | solution.py:519
  184.9 8.2 %collective-permute-start.10 = (f32[2,4,64,128]{3,2,1,0:T(8,128)S(1)}, f32[2,4,64,128]{3,2,1,0:T(8,128)S(1)}, u32[]{:S(2)}, u32[]{:S(2)}) collective-permute-start(f32[2,4,64,128]{3,2,1,0:T(8,128)S(1)} %slice.11), channel_id=1, source_target_pairs={{6,0},{7,1},{0,2},{1,3},{2,4},{3,5},{4,6},{5,7},{14,8},{15,9},{8,1... | collective-permute-start | bytes 786440 | tf_op jit(solution)/shard_map/ppermute | solution.py:520
  185.9 10.2 %collective-permute-start.12 = (f32[4,4,64,128]{3,2,1,0:T(8,128)S(1)}, f32[4,4,64,128]{3,2,1,0:T(8,128)S(1)}, u32[]{:S(2)}, u32[]{:S(2)}) collective-permute-start(f32[4,4,64,128]{3,2,1,0:T(8,128)S(1)} %collective-permute-done.7.refs_1_), channel_id=1, source_target_pairs={{0,1},{1,0},{2,3},{3,2},{4,5},{5,4},{6,7},{7,6},{8,9},{9,8},{10,11... | collective-permute-start | bytes 1572872 | tf_op jit(solution)/shard_map/ppermute | solution.py:523
  188.2 9.4 %collective-permute-start.13 = (f32[4,4,64,128]{3,2,1,0:T(8,128)S(1)}, f32[4,4,64,128]{3,2,1,0:T(8,128)}, u32[]{:S(2)}, u32[]{:S(2)}) collective-permute-start(f32[4,4,64,128]{3,2,1,0:T(8,128)S(1)} %collective-permute-done.8.refs_2_), channel_id=1, source_target_pairs={{0,1},{1,0},{2,3},{3,2},{4,5},{5,4},{6,7},{7,6},{8,9},{9,8},{10,11... | collective-permute-start | bytes 1572872 | tf_op jit(solution)/shard_map/ppermute | solution.py:523
  190.5 7.2 %copy-start.6 = (f32[2,4,64,128]{3,2,1,0:T(8,128)}, f32[2,4,64,128]{3,2,1,0:T(8,128)S(1)}, u32[]{:S(2)}) copy-start(f32[2,4,64,128]{3,2,1,0:T(8,128)S(1)} %collective-permute-done.9.refs_3_) | copy-start | bytes 786436
  190.5 5.6 %collective-permute-start.14 = (f32[2,4,64,128]{3,2,1,0:T(8,128)S(1)}, f32[2,4,64,128]{3,2,1,0:T(8,128)}, u32[]{:S(2)}, u32[]{:S(2)}) collective-permute-start(f32[2,4,64,128]{3,2,1,0:T(8,128)S(1)} %collective-permute-done.9.refs_3_), channel_id=1, source_target_pairs={{0,1},{1,0},{2,3},{3,2},{4,5},{5,4},{6,7},{7,6},{8,9},{9,8},{10,11... | collective-permute-start | bytes 786440 | tf_op jit(solution)/shard_map/ppermute | solution.py:523
  193.1 3.1 %copy-start.7 = (f32[2,4,64,128]{3,2,1,0:T(8,128)}, f32[2,4,64,128]{3,2,1,0:T(8,128)S(1)}, u32[]{:S(2)}) copy-start(f32[2,4,64,128]{3,2,1,0:T(8,128)S(1)} %collective-permute-done.10.refs_4_) | copy-start | bytes 786436
  193.1 3.0 %collective-permute-start.15 = (f32[2,4,64,128]{3,2,1,0:T(8,128)S(1)}, f32[2,4,64,128]{3,2,1,0:T(8,128)}, u32[]{:S(2)}, u32[]{:S(2)}) collective-permute-start(f32[2,4,64,128]{3,2,1,0:T(8,128)S(1)} %collective-permute-done.10.refs_4_), channel_id=1, source_target_pairs={{0,1},{1,0},{2,3},{3,2},{4,5},{5,4},{6,7},{7,6},{8,9},{9,8},{10,11... | collective-permute-start | bytes 786440 | tf_op jit(solution)/shard_map/ppermute | solution.py:523
  196.1 0.8 copy-start.3
  196.8 0.8 copy-start.4
Sparse Core Ops, SparseCore 0:
  136.1 44.5 all-gather.6
  182.9 75.3 all-gather.4

commit v3 on v2

v3 whole, which is shorter than its diff:
```python
import jax
import jax.numpy as jnp
from jax import lax
from jax.experimental import pallas as pl
from jax.experimental.pallas import tpu as pltpu
from jax.sharding import PartitionSpec as P

B = 128
HB = 64
ROWS = 16
COLS = 8
HALF = 8
LR = 8
LC = 16
CB = 8
PANEL = 1024
f32 = jnp.float32
bf16 = jnp.bfloat16
exact = lax.Precision.HIGHEST
MIB = 2**20
VMEM = 62 * MIB
CHEAP = pl.CostEstimate(flops=2**10, bytes_accessed=2**10, transcendentals=0)


def block_dot(left, right, contract_left=1):
    dims = (((contract_left,), (0,)), ((), ()))
    return lax.dot_general(left, right, dims, preferred_element_type=f32)


def exact_dot(left, right, contract_left=1):
    dims = (((contract_left,), (0,)), ((), ()))
    return lax.dot_general(left, right, dims, precision=exact, preferred_element_type=f32)


def split(value):
    high = value.astype(bf16)
    return high, (value - high.astype(f32)).astype(bf16)


def pack_slots(child, table, second):
    def body(tab, child_ref, out_ref, held, packed, zero, in_sem, out_sem):
        halves = (1,) if second else (0, 1)
        size = len(halves)

        def fetch(i, n):
            return pltpu.make_async_copy(
                child_ref.at[i, :, halves[n]], held.at[i, n], in_sem.at[i, n]
            )

        for i in range(CB):
            for n in range(size):
                fetch(i, n).start()
        zero[...] = jnp.zeros_like(zero)
        for i in range(CB):
            parent = tab[i]
            mine = parent % ROWS
            other = (mine + HALF) % ROWS
            for n in range(size):
                fetch(i, n).wait()
                for place in range(COLS):
                    source = tab[CB + place]
                    gain = tab[2 * CB + i * CB + source].astype(f32)
                    packed[i, n, place] = held[i, n, source] * gain
            pltpu.make_async_copy(packed.at[i, 0], out_ref.at[mine], out_sem.at[i, 0]).start()
            if second:
                pltpu.make_async_copy(zero, out_ref.at[other], out_sem.at[i, 1]).start()
            else:

                @pl.when(parent < HALF)
                def _():
                    pltpu.make_async_copy(
                        packed.at[i, 1], out_ref.at[other], out_sem.at[i, 1]
                    ).start()

                @pl.when(parent >= HALF)
                def _():
                    pltpu.make_async_copy(zero, out_ref.at[other], out_sem.at[i, 1]).start()

        for i in range(CB):
            for n in range(2):
                pltpu.make_async_copy(zero, out_ref.at[0], out_sem.at[i, n]).wait()

    size = 1 if second else 2
    return pl.pallas_call(
        body,
        in_specs=[
            pl.BlockSpec(memory_space=pltpu.SMEM),
            pl.BlockSpec(memory_space=pl.ANY),
        ],
        out_specs=pl.BlockSpec(memory_space=pl.ANY),
        out_shape=jax.ShapeDtypeStruct((ROWS, COLS, HB, B), f32),
        scratch_shapes=[
            pltpu.VMEM((CB, size, CB, HB, B), f32),
            pltpu.VMEM((CB, size, COLS, HB, B), f32),
            pltpu.VMEM((COLS, HB, B), f32),
            pltpu.SemaphoreType.DMA((CB, size)),
            pltpu.SemaphoreType.DMA((CB, 2)),
        ],
        compiler_params=pltpu.CompilerParams(vmem_limit_bytes=VMEM),
        cost_estimate=CHEAP,
    )(table, child)


def gain_of(code):
    return (code > 0).astype(f32)


def place_of(code):
    return jnp.maximum(code - 1, 0)


NKEYS = LR + 1 + LC


def leading_row(front, received, arrived, table):
    def body(tab, own_ref, recv_ref, first_ref, other_ref, top_ref, even_ref, odd_ref, lead_ref):
        upper = tab[2 * NKEYS] < HALF
        side = tab[2 * NKEYS] // HALF
        for m in range(LC):
            value = jnp.where(upper, own_ref[0, m, 0], recv_ref[m])
            for child, ref in ((0, first_ref), (1, other_ref)):
                base = child * NKEYS
                code = tab[base + LR + 1 + m]
                gain = gain_of(code) * gain_of(tab[base + LR])
                value = value + ref[0, place_of(code)] * gain
            top_ref[m] = value
        lead_ref[...] = top_ref[0]
        for l in range(LR):
            even_ref[l] = top_ref[2 * l + side]
            odd_ref[l] = top_ref[2 * l + 1 - side]

    def rows_of(child):
        return lambda step, tab: (child * HALF + place_of(tab[child * NKEYS + LR]), 0, 0, 0)

    return pl.pallas_call(
        body,
        grid_spec=pltpu.PrefetchScalarGridSpec(
            num_scalar_prefetch=1,
            grid=(1,),
            in_specs=[
                pl.BlockSpec((1, LC, 1, HB, B), lambda step, tab: (0, 0, 0, 0, 0)),
                pl.BlockSpec((LC, HB, B), lambda step, tab: (0, 0, 0)),
                pl.BlockSpec((1, COLS, HB, B), rows_of(0)),
                pl.BlockSpec((1, COLS, HB, B), rows_of(1)),
            ],
            out_specs=[
                pl.BlockSpec((LC, HB, B), lambda step, tab: (0, 0, 0)),
                pl.BlockSpec((LR, HB, B), lambda step, tab: (0, 0, 0)),
                pl.BlockSpec((LR, HB, B), lambda step, tab: (0, 0, 0)),
                pl.BlockSpec((HB, B), lambda step, tab: (0, 0)),
            ],
        ),
        out_shape=[
            jax.ShapeDtypeStruct((LC, HB, B), f32),
            jax.ShapeDtypeStruct((LR, HB, B), f32),
            jax.ShapeDtypeStruct((LR, HB, B), f32),
            jax.ShapeDtypeStruct((HB, B), f32),
        ],
        compiler_params=pltpu.CompilerParams(vmem_limit_bytes=VMEM),
        cost_estimate=CHEAP,
    )(table, front, received, arrived, arrived)


def extend_add(front, arrived, table, half):
    def body(tab, parent_ref, first_ref, other_ref, out_ref):
        step = pl.program_id(0)
        for m in range(LC):
            value = parent_ref[0, m, 0]
            for child, ref in ((0, first_ref), (1, other_ref)):
                base = child * NKEYS
                code = tab[base + LR + 1 + m]
                gain = gain_of(code) * gain_of(tab[base + step])
                value = value + ref[0, place_of(code)] * gain
            out_ref[0, m] = value

    def rows_of(child):
        return lambda step, tab: (child * HALF + place_of(tab[child * NKEYS + step]), 0, 0, 0)

    return pl.pallas_call(
        body,
        grid_spec=pltpu.PrefetchScalarGridSpec(
            num_scalar_prefetch=1,
            grid=(LR,),
            in_specs=[
                pl.BlockSpec((1, LC, 1, HB, B), lambda step, tab: (step, 0, half, 0, 0)),
                pl.BlockSpec((1, COLS, HB, B), rows_of(0)),
                pl.BlockSpec((1, COLS, HB, B), rows_of(1)),
            ],
            out_specs=pl.BlockSpec((1, LC, HB, B), lambda step, tab: (step, 0, 0, 0)),
        ),
        out_shape=jax.ShapeDtypeStruct((LR, LC, HB, B), f32),
        compiler_params=pltpu.CompilerParams(vmem_limit_bytes=VMEM),
        cost_estimate=CHEAP,
    )(table, front, arrived, arrived)


def factor_block(block):
    lane = lax.broadcasted_iota(jnp.int32, (8, B), 1)
    sub = lax.broadcasted_iota(jnp.int32, (8, B), 0)

    def lanes(tile, j):
        return jnp.broadcast_to(tile[:, j : j + 1], (8, B))

    def subs(tile, k):
        return jnp.broadcast_to(tile[k : k + 1, :], (8, B))

    tiles = [block[8 * r : 8 * r + 8, :] for r in range(B // 8)]
    for group in range(B // 8):
        low = 8 * group
        own = [lanes(tiles[group], low + k) for k in range(8)]
        work = tiles[group]
        inside = jnp.logical_and(lane >= low, lane < low + 8)
        upper = []
        for k in range(0, 8, 2):
            n = k + 1
            a, b, c = subs(own[k], k), subs(own[n], k), subs(own[n], n)
            det = 1.0 / (a * c - b * b)
            at_k, at_n = lane == low + k, lane == low + n
            on_k, on_n = sub == k, sub == n
            on = jnp.logical_or(on_k, on_n)
            row_k, row_n = subs(work, k), subs(work, n)
            upper.append(row_k)
            ratio = b * (1.0 / a)
            upper.append(jnp.where(at_k, 0.0, row_n) - ratio * jnp.where(at_k, 1.0, row_k))
            row_k = jnp.where(at_k, 1.0, jnp.where(at_n, 0.0, row_k))
            row_n = jnp.where(at_n, 1.0, jnp.where(at_k, 0.0, row_n))
            new_k = det * (c * row_k - b * row_n)
            new_n = det * (a * row_n - b * row_k)
            coef_k = jnp.where(on_k, -1.0, jnp.where(on_n, 0.0, own[k]))
            coef_n = jnp.where(on_n, -1.0, jnp.where(on_k, 0.0, own[n]))
            clear = jnp.logical_or(jnp.logical_or(at_k, at_n), on)
            work = jnp.where(clear, 0.0, work) - coef_k * new_k - coef_n * new_n
            for m in range(k + 2, 8):
                x, y = subs(own[m], k), subs(own[m], n)
                step = coef_k * (det * (c * x - b * y)) + coef_n * (det * (a * y - b * x))
                own[m] = jnp.where(on, 0.0, own[m]) - step
        solved = [subs(work, k) for k in range(8)]
        rows = upper[0]
        for k in range(1, 8):
            rows = jnp.where(sub == k, upper[k], rows)
        tiles[group] = rows
        for r in range(group + 1, B // 8):
            value = jnp.where(inside, 0.0, tiles[r])
            for k in range(8):
                value = value - lanes(tiles[r], low + k) * solved[k]
            tiles[r] = value
    return jnp.concatenate(tiles, axis=0)


def factor_and_solve(pieces, where):
    def origin(at, n):
        dk, dy = n // 5, (0, 1, 3, 2, 2)[n % 5]
        return ((at[2] + dy) % 4) * 2 + (at[3] + dk) % 2

    def body(at, *refs):
        lead_refs, rows_refs, refs = refs[:10], refs[10:20], refs[20:]
        high_ref, low_ref, out_ref, w, diag, rows, gh, gl, wh, wl, below, bh, bl, sem = refs
        p = at[0] * 4 + at[1]
        q = at[2] * 2 + at[3]
        side = p // HALF
        copies = []
        for n, ref in enumerate(rows_refs):
            e = origin(at, n) ^ (p % HALF)
            for half in range(ref.shape[0]):
                order = 1 if n % 5 == 4 else half
                copies.append(
                    pltpu.make_async_copy(ref.at[half, 1], rows.at[e, order], sem.at[e, order])
                )
        for copy in copies:
            copy.start()
        for n, ref in enumerate(lead_refs):
            e = origin(at, n)
            for half in range(ref.shape[0]):
                for place in range(LR):
                    dx = half * 2 + place // 4 + (2 if n % 5 == 4 else 0)
                    x, z = (at[0] + dx) % 4, (at[1] + place) % 4
                    g = (x % 2) * 4 + z
                    top = pl.multiple_of(g * B + (x // 2) * HB, HB)
                    w[pl.ds(top, HB), pl.ds(pl.multiple_of(e * B, B), B)] = ref[half, 0, place]
        row = lax.broadcasted_iota(jnp.int32, (B, B), 0)
        col = lax.broadcasted_iota(jnp.int32, (B, B), 1)
        def step(kb, carry):
            o = pl.multiple_of(kb * B, B)
            f = factor_block(w[pl.ds(o, B), pl.ds(o, B)])
            pivots = jnp.sum(jnp.where(row == col, f, 0.0), axis=1, keepdims=True)
            scale = 1.0 / jnp.sqrt(pivots)
            inverse = jnp.where(row > col, f, (row == col).astype(f32)) * scale
            diag[pl.ds(o, B), :] = jnp.where(row <= col, f, 0.0) * scale
            w[pl.ds(o, B), :] = exact_dot(inverse, w[pl.ds(o, B), :])
            w[pl.ds(o, B), pl.ds(o, B)] = inverse

            @pl.when(kb % 2 == 0)
            def _():
                n = pl.multiple_of(o + B, B)
                w[pl.ds(n, B), pl.ds(o, B)] = jnp.zeros((B, B), f32)
                w[pl.ds(n, B), :] -= exact_dot(w[pl.ds(o, B), pl.ds(n, B)], w[pl.ds(o, B), :], 0)

            for done in range(256, PANEL, 256):

                @pl.when(kb == done // B - 1)
                def _():
                    above = (slice(done - 256, done - B), slice(done - B, done))
                    kept = w[above]
                    w[above] = jnp.zeros((B, B), f32)
                    w[done:, done - 256 : done] = jnp.zeros((PANEL - done, 256), f32)
                    for n in range(done, PANEL, 256):
                        left = w[done - 256 : done, n : n + 256]
                        w[n : n + 256, :] -= exact_dot(left, w[done - 256 : done, :], 0)
                    w[above] = kept

            return carry

        lax.fori_loop(0, PANEL // B, step, 0)

        for copy in copies:
            copy.wait()
        for e in range(COLS):
            for order in range(2):
                half = side if order == 0 else 1 - side
                top = pl.multiple_of(e * B + half * HB, HB)
                for l in range(LR):
                    high, low = split(rows[e, order, l])
                    gh[pl.ds(top, HB), l * B : (l + 1) * B] = high
                    gl[pl.ds(top, HB), l * B : (l + 1) * B] = low
        for r in range(0, PANEL, 256):
            shape = (256, r + 256)
            under = (
                lax.broadcasted_iota(jnp.int32, shape, 0) + r
                >= lax.broadcasted_iota(jnp.int32, shape, 1)
            )
            high, low = split(jnp.where(under, w[r : r + 256, : r + 256], 0.0))
            wh[r : r + 256, : r + 256] = high
            wl[r : r + 256, : r + 256] = low
            value = block_dot(high, gh[: r + 256, :])
            value += block_dot(high, gl[: r + 256, :])
            value += block_dot(low, gh[: r + 256, :])
            for l in range(LR):
                for n in range(0, 256, B):
                    tile = value[n : n + B, l * B : (l + 1) * B].T
                    high, low = split(tile)
                    place = (slice(l * B, (l + 1) * B), slice(r + n, r + n + B))
                    below[place] = tile
                    bh[place] = high
                    bl[place] = low
        mine = pl.ds(pl.multiple_of(q * B, B), B)
        for l in range(LR):
            out_ref[l] = below[l * B : (l + 1) * B, mine]

        @pl.when(p < HALF)
        def _():
            over = w[mine, pl.ds(pl.multiple_of((p % HALF) * B, B), B)]
            top = jnp.where(p > q, over, jnp.where(p == q, diag[mine, :], 0.0))
            out_ref[0] = top.T

        for r in range(0, PANEL, 256):
            value = block_dot(bh[:, r:], wh[r:, r : r + 256])
            value += block_dot(bl[:, r:], wh[r:, r : r + 256])
            value += block_dot(bh[:, r:], wl[r:, r : r + 256])
            high, low = split(value)
            high_ref[:, r : r + 256] = high
            low_ref[:, r : r + 256] = low

        @pl.when(p < HALF)
        def _():
            high_ref[:B, :] = jnp.zeros((B, PANEL), bf16)
            low_ref[:B, :] = jnp.zeros((B, PANEL), bf16)

    whole = pl.BlockSpec((PANEL, PANEL), lambda step: (0, 0))
    return pl.pallas_call(
        body,
        grid=(1,),
        in_specs=[pl.BlockSpec(memory_space=pltpu.SMEM)]
        + [
            pl.BlockSpec((piece.shape[0], 1, LR, HB, B), lambda step: (0, 0, 0, 0, 0))
            for piece in pieces
        ]
        + [pl.BlockSpec(memory_space=pl.ANY)] * 10,
        out_specs=[whole, whole, pl.BlockSpec((LR, B, B), lambda step: (0, 0, 0))],
        out_shape=[
            jax.ShapeDtypeStruct((PANEL, PANEL), bf16),
            jax.ShapeDtypeStruct((PANEL, PANEL), bf16),
            jax.ShapeDtypeStruct((LR, B, B), f32),
        ],
        scratch_shapes=[
            pltpu.VMEM((PANEL, PANEL), f32),
            pltpu.VMEM((PANEL, B), f32),
            pltpu.VMEM((COLS, 2, LR, HB, B), f32),
            pltpu.VMEM((PANEL, PANEL), bf16),
            pltpu.VMEM((PANEL, PANEL), bf16),
            pltpu.VMEM((PANEL, PANEL), bf16),
            pltpu.VMEM((PANEL, PANEL), bf16),
            pltpu.VMEM((PANEL, PANEL), f32),
            pltpu.VMEM((PANEL, PANEL), bf16),
            pltpu.VMEM((PANEL, PANEL), bf16),
            pltpu.SemaphoreType.DMA((COLS, 2)),
        ],
        compiler_params=pltpu.CompilerParams(vmem_limit_bytes=VMEM),
        cost_estimate=CHEAP,
    )(where, *pieces, *pieces)


def trailing_update(table, upper, front, second, columns, high, low, panel):
    steps = LC // 2

    def body(tab, upper_ref, front_ref, second_ref, col_ref, high_ref, low_ref, panel_ref, out_ref,
             ch, cl, got, sem):
        step = pl.program_id(0)
        slot = step % 2

        def fetch(step, slot):
            for child in range(2):
                base = child * NKEYS
                for l in range(LR):
                    source = child * HALF + place_of(tab[base + l])
                    for n in range(2):
                        place = place_of(tab[base + LR + 1 + 2 * step + n])
                        pltpu.make_async_copy(
                            second_ref.at[source, place], got.at[slot, child, l, n], sem.at[slot]
                        ).start()

        @pl.when(step == 0)
        def _():
            fetch(step, slot)

        @pl.when(step + 1 < steps)
        def _():
            fetch(step + 1, 1 - slot)

        for p in range(ROWS):
            top = (p % HALF) * B + (p // HALF) * HB
            for n in range(2):
                hi, lo = split(col_ref[p, n])
                ch[top : top + HB, n * B : (n + 1) * B] = hi
                cl[top : top + HB, n * B : (n + 1) * B] = lo
        pltpu.make_async_copy(got.at[slot], got.at[slot], sem.at[slot]).wait()
        for r in range(0, PANEL, 256):
            value = block_dot(high_ref[r : r + 256, :], ch[...])
            value += block_dot(high_ref[r : r + 256, :], cl[...])
            value += block_dot(low_ref[r : r + 256, :], ch[...])
            for l in range(r // B, r // B + 2):
                for n in range(2):
                    s = l * B - r
                    cols = slice(n * B, (n + 1) * B)
                    out_ref[l, n, :HB] = upper_ref[l, n] - value[s : s + HB, cols]
                    total = front_ref[l, n, 0]
                    for child in range(2):
                        base = child * NKEYS
                        gain = gain_of(tab[base + LR + 1 + 2 * step + n]) * gain_of(tab[base + l])
                        total = total + got[slot, child, l, n] * gain
                    out_ref[l, n, HB:] = total - value[s + HB : s + B, cols]

        @pl.when(step == 0)
        def _():
            for l in range(LR):
                out_ref[l, 0] = panel_ref[l]

    whole = pl.BlockSpec((PANEL, PANEL), lambda step, tab: (0, 0))
    return pl.pallas_call(
        body,
        grid_spec=pltpu.PrefetchScalarGridSpec(
            num_scalar_prefetch=1,
            grid=(steps,),
            in_specs=[
                pl.BlockSpec((LR, 2, HB, B), lambda step, tab: (0, step, 0, 0)),
                pl.BlockSpec((LR, 2, 1, HB, B), lambda step, tab: (0, step, 1, 0, 0)),
                pl.BlockSpec(memory_space=pl.ANY),
                pl.BlockSpec((ROWS, 2, HB, B), lambda step, tab: (0, step, 0, 0)),
                whole,
                whole,
                pl.BlockSpec((LR, B, B), lambda step, tab: (0, 0, 0)),
            ],
            out_specs=pl.BlockSpec((LR, 2, B, B), lambda step, tab: (0, step, 0, 0)),
            scratch_shapes=[
                pltpu.VMEM((PANEL, 256), bf16),
                pltpu.VMEM((PANEL, 256), bf16),
                pltpu.VMEM((2, 2, LR, 2, HB, B), f32),
                pltpu.SemaphoreType.DMA((2,)),
            ],
        ),
        out_shape=jax.ShapeDtypeStruct((LR, LC, B, B), f32),
        compiler_params=pltpu.CompilerParams(vmem_limit_bytes=VMEM),
        cost_estimate=CHEAP,
    )(table, upper, front, second, columns, high, low, panel)


def along_x(distance):
    return [(4 * ((x + distance) % 4) + z, 4 * x + z) for x in range(4) for z in range(4)]


def along_z(distance):
    return [(4 * x + (z + distance) % 4, 4 * x + z) for x in range(4) for z in range(4)]


def along_y(distance):
    return [(2 * ((y + distance) % 4) + k, 2 * y + k) for y in range(4) for k in range(2)]


OTHER_CORE = [(q, q ^ 1) for q in range(COLS)]


def transposed(same):
    pairs = []
    for p in range(ROWS):
        for q in range(COLS):
            side = p // HALF if same else 1 - p // HALF
            pairs.append((p * COLS + q, (q + HALF * side) * COLS + (p % HALF ^ q)))
    return pairs


def shards(parent_front, child_updates, child_mask, child_map):
    p = lax.axis_index("row")
    q = lax.axis_index("col")
    both = ("row", "col")
    front = parent_front.reshape(LR, LC, 2, HB, B)
    child = child_updates.reshape(CB, CB, 2, HB, B)

    own_map = child_map[p // HALF].reshape(CB, CB)
    row_parent = own_map[:, p % HALF]
    col_parent = own_map[:, q]
    index = jnp.arange(CB)
    column = jnp.sum((col_parent[None] % COLS == index[:, None]) * index[None], axis=1)
    source_table = jnp.concatenate([row_parent, column, child_mask.reshape(-1)]).astype(jnp.int32)

    keys = jnp.concatenate(
        [jnp.arange(LR) * ROWS + p, (p % HALF)[None], jnp.arange(LC) * COLS + q]
    )
    hits = child_map[:, None, :] == keys[None, :, None]
    codes = jnp.sum(hits * (jnp.arange(CB * CB) % CB + 1)[None, None], axis=2)
    target_table = jnp.concatenate([codes.reshape(-1), p[None]]).astype(jnp.int32)

    top_other = lax.ppermute(front[0, :, 1], "row", [(i, i + HALF) for i in range(HALF)])

    first = pack_slots(child, source_table, False)
    first = lax.all_to_all(
        first.reshape(ROWS * COLS, HB, B), both, 0, 0, tiled=True
    ).reshape(ROWS, COLS, HB, B)
    second = pack_slots(child, source_table, True)

    first, second = lax.optimization_barrier((first, second))
    target_table, top_other = lax.optimization_barrier((target_table, top_other))
    top, even, odd, lead = leading_row(front, top_other, first, target_table)

    turned = [
        lax.ppermute(even, both, transposed(True)),
        lax.ppermute(odd, both, transposed(False)),
    ]
    near = [lead] + [lax.ppermute(lead, "row", along_z(d)) for d in range(1, 4)]
    stacked = jnp.stack(near)
    near = [stacked] + [lax.ppermute(stacked, "row", along_x(d)) for d in range(1, 4)]
    packed = jnp.stack(
        [jnp.concatenate(near[:2]), turned[0], jnp.concatenate(near[2:]), turned[1]]
    ).reshape(2, 2, LR, HB, B)
    top, packed = lax.optimization_barrier((top, packed))

    columns = lax.all_gather(top, "row", axis=0)

    ahead = lax.ppermute(packed, "col", along_y(1))
    back = lax.ppermute(packed, "col", along_y(3))
    upper = extend_add(front, first, target_table, 0)
    upper, ahead, back = lax.optimization_barrier((upper, ahead, back))
    far = [
        lax.ppermute(ahead[:1], "col", along_y(1)),
        lax.ppermute(back[1:], "col", along_y(3)),
    ]
    second, far[0], far[1] = lax.optimization_barrier((second, far[0], far[1]))
    near = [packed, ahead, back] + far
    near = near + [lax.ppermute(piece, "col", OTHER_CORE) for piece in near]

    second = lax.all_to_all(
        second.reshape(ROWS * COLS, HB, B), both, 0, 0, tiled=True
    ).reshape(ROWS, COLS, HB, B)

    where = jnp.stack([p // 4, p % 4, q // 2, q % 2]).astype(jnp.int32)
    high, low, panel = factor_and_solve(near, where)
    high, columns = lax.optimization_barrier((high, columns))
    return trailing_update(target_table, upper, front, second, columns, high, low, panel)


def solution(mesh):
    in_specs = (P("row", "col", None, None), P("row", "col", None, None), P("row", "col"), P())
    out_specs = P("row", "col", None, None)
    return jax.shard_map(shards, mesh=mesh, in_specs=in_specs, out_specs=out_specs, check_vma=False)
```

time: 291 us -> 272 us (0.935)
  waiting for transfers between devices: 114 us -> 86.7 us
  starting transfers between devices: 45.9 us -> 55.6 us
  Pallas kernels: 107 us -> 103 us
  local copies, waits for them, and re-layouts: 4.56 us -> 7.88 us
    ppermute x1, waiting for transfers between devices: 94.4 us -> 43.1 us  [shards(): lax.ppermute(front[0, :, 1], 'row', [(i, i + HALF) for i in range(HALF)])]
    ppermute x4 -> x6, waiting for transfers between devices: 5.51 us -> 28.1 us  [the longest x1 14.9 us: shards(): back = lax.ppermute(packed, 'col', along_y(3))]
    ppermute x4 -> x6, starting transfers between devices: 3.13 us -> 16.7 us  [the longest x1 5.21 us: shards(): lax.ppermute(odd, both, transposed(False))]
    all_to_all x1 -> x2, starting transfers between devices: 12 us -> 21.3 us  [the longest x1 12 us: shards(): lax.all_to_all(first.reshape(ROWS * COLS, HB, B), both, 0, 0, tiled=True)]
    ppermute x5, starting transfers between devices: 10.7 us -> 2.24 us  [shards(): near = near + [lax.ppermute(piece, 'col', OTHER_CORE) for piece in near]]
    ppermute x3, starting transfers between devices: 11.4 us -> 5.76 us  [shards(): lax.ppermute(stacked, 'row', along_x(d))]
    pallas_call x4 -> x2, Pallas kernels: 88.3 us -> 83.2 us  [the longest x1 59.9 us: factor_and_solve(): pl.pallas_call(body, grid=(1,), in_specs=[pl.BlockSpec(memory_space=pltpu...]
    ppermute x3, waiting for transfers between devices: 6.16 us -> 11 us  [shards(): lax.ppermute(stacked, 'row', along_x(d))]
  transfers between devices with their start and end apart: 19 -> 21, of which waited for: 12 -> 10; matrix products, arithmetic and copies ran while one was open for 2% -> 3% of each run, Pallas kernels for 28% -> 27%
where the time goes in v3:
time: 272 us; the launch traced here: 270 us
  Pallas kernels  103 us (38%)
  waiting for transfers between devices  86.7 us (32%)
  starting transfers between devices  55.6 us (20%)
  between operations  13.6 us (5%)
  local copies, waits for them, and re-layouts  7.88 us (3%)
  other arithmetic  3.58 us (1%)
    pallas_call x1, Pallas kernels, factor_and_solve(): pl.pallas_call(body, grid=(1,), in_specs=[pl.BlockSpec(memory_space=pltpu...  59.9 us
    ppermute x1, waiting for transfers between devices, shards(): lax.ppermute(front[0, :, 1], 'row', [(i, i + HALF) for i in range(HALF)])  43.1 us
    pallas_call x1, Pallas kernels, trailing_update(): pl.pallas_call(body, grid_spec=pltpu.PrefetchScalarGridSpec(num_scalar_pr...  23.3 us
    ppermute x1, waiting for transfers between devices, shards(): back = lax.ppermute(packed, 'col', along_y(3))  14.9 us
    all_to_all x1, starting transfers between devices, shards(): lax.all_to_all(first.reshape(ROWS * COLS, HB, B), both, 0, 0, tiled=True)  12 us
    ppermute x3, waiting for transfers between devices, shards(): lax.ppermute(stacked, 'row', along_x(d))  11 us
    all_to_all x1, starting transfers between devices, shards(): lax.all_to_all(second.reshape(ROWS * COLS, HB, B), both, 0, 0, tiled=True)  9.29 us
    ppermute x1, waiting for transfers between devices, shards(): lax.ppermute(ahead[:1], 'col', along_y(1))  9.11 us
  transfers between devices with their start and end apart: 21, of which 10 were waited for; matrix products, arithmetic and copies ran while one was open for 3% of the time, Pallas kernels for 27%

profile of v3, /device:TPU:1, one launch (start us, length us, event | category | flops | bytes accessed | tf_op | source)
XLA Modules:
  0.0 270.3 jit_solution(14333641791691572602)
XLA Ops:
  9.0 4.4 %shard_map.46 = f32[16,8,64,128]{3,2,1,0:T(8,128)} custom-call(s32[80]{0:T(128)} %pad_add_fusion.2.tab, f32[8,8,2,64,128]{4,3,2,1,0:T(8,128)} %bitcast.33), custom_call_target="tpu_custom_call" | custom-call | flops 1024 | bytes 1024 | tf_op jit(solution)/shard_map/pallas_call | solution.py:84
  13.4 12.0 %all-to-all-start = ((f32[128,64,128]{2,1,0:T(8,128)}), f32[128,64,128]{2,1,0:T(8,128)}, u32[]{:S(2)}, u32[]{:S(2)}) async-start(f32[128,64,128]{2,1,0:T(8,128)} %bitcast.36), calls=%async_computation | async-start | bytes 8388608 | tf_op jit(solution)/shard_map/all_to_all | solution.py:534
  25.4 1.1 slice_bitcast_fusion
  26.5 4.8 %collective-permute-start = (f32[16,64,128]{2,1,0:T(8,128)S(1)}, f32[16,64,128]{2,1,0:T(8,128)S(1)}, u32[]{:S(2)}, u32[]{:S(2)}) collective-permute-start(f32[16,64,128]{2,1,0:T(8,128)S(1)} %slice_bitcast_fusion), channel_id=1, source_target_pairs={{0,64},{8,72},{16,80},{24,88},{32,96},{40,104},{48,112},{56,120},{... | collective-permute-start | bytes 1572872 | tf_op jit(solution)/shard_map/ppermute | solution.py:531
  31.4 3.8 %shard_map.47 = f32[16,8,64,128]{3,2,1,0:T(8,128)} custom-call(s32[80]{0:T(128)} %pad_add_fusion.2.tab, f32[8,8,2,64,128]{4,3,2,1,0:T(8,128)} %bitcast.34), custom_call_target="tpu_custom_call" | custom-call | flops 1024 | bytes 1024 | tf_op jit(solution)/shard_map/pallas_call | solution.py:84
  36.7 43.1 %collective-permute-done.recv_ref = f32[16,64,128]{2,1,0:T(8,128)S(1)} collective-permute-done((f32[16,64,128]{2,1,0:T(8,128)S(1)}, f32[16,64,128]{2,1,0:T(8,128)S(1)}, u32[]{:S(2)}, u32[]{:S(2)}) %collective-permute-start) | collective-permute-done | bytes 524320 | tf_op jit(solution)/shard_map/ppermute | solution.py:531
  79.8 0.8 copy-done.3
  80.7 3.1 %shard_map.49 = (f32[16,64,128]{2,1,0:T(8,128)}, f32[8,64,128]{2,1,0:T(8,128)}, f32[8,64,128]{2,1,0:T(8,128)}, f32[64,128]{1,0:T(8,128)}) custom-call(s32[51]{0:T(128)} %pad_add_fusion.1.tab, f32[8,16,2,64,128]{4,3,2,1,0:T(8,128)} %bitcast.30, f32[16,64,128]{2,1,0:T(8,128)} %copy-done.3, f32[16,8,64,128]{3,2,1,0:T(8,128)} %bitcast.6.first_ref.other_ref, ...), custom_call_target="tpu_custom_call" | custom-call | flops 1024 | bytes 1024 | tf_op jit(solution)/shard_map/pallas_call | solution.py:135
  83.8 3.9 %collective-permute-start.1 = (f32[64,128]{1,0:T(8,128)}, f32[64,128]{1,0:T(8,128)S(1)}, u32[]{:S(2)}, u32[]{:S(2)}) collective-permute-start(f32[64,128]{1,0:T(8,128)} %get-tuple-element.30), channel_id=1, source_target_pairs={{8,0},{16,8},{24,16},{0,24},{40,32},{48,40},{56,48},{32,56},{72,64... | collective-permute-start | bytes 98312 | tf_op jit(solution)/shard_map/ppermute | solution.py:547
  88.5 0.8 constant_dynamic-update-slice_fusion.4
  89.3 3.7 %collective-permute-start.5 = (f32[8,64,128]{2,1,0:T(8,128)}, f32[8,64,128]{2,1,0:T(8,128)S(1)}, u32[]{:S(2)}, u32[]{:S(2)}) collective-permute-start(f32[8,64,128]{2,1,0:T(8,128)} %get-tuple-element.31), channel_id=1, source_target_pairs={{0,0},{1,9},{2,18},{3,27},{4,36},{5,45},{6,54},{7,63},{8,1},{9,8},... | collective-permute-start | bytes 786440 | tf_op jit(solution)/shard_map/ppermute | solution.py:544
  93.0 5.2 %collective-permute-start.8 = (f32[8,64,128]{2,1,0:T(8,128)}, f32[8,64,128]{2,1,0:T(8,128)S(1)}, u32[]{:S(2)}, u32[]{:S(2)}) collective-permute-start(f32[8,64,128]{2,1,0:T(8,128)} %get-tuple-element.32), channel_id=1, source_target_pairs={{0,64},{1,73},{2,82},{3,91},{4,100},{5,109},{6,118},{7,127},{8,65}... | collective-permute-start | bytes 786440 | tf_op jit(solution)/shard_map/ppermute | solution.py:545
  99.0 2.7 collective-permute-start.4
  101.7 3.1 %collective-permute-start.6 = (f32[4,64,128]{2,1,0:T(8,128)S(1)}, f32[4,64,128]{2,1,0:T(8,128)S(1)}, u32[]{:S(2)}, u32[]{:S(2)}) collective-permute-start(f32[4,64,128]{2,1,0:T(8,128)S(1)} %pad_maximum_fusion.1), channel_id=1, source_target_pairs={{64,0},{72,8},{80,16},{88,24},{96,32},{104,40},{112,48},{120,56},{... | collective-permute-start | bytes 393224 | tf_op jit(solution)/shard_map/ppermute | solution.py:549
  104.8 2.0 collective-permute-done.4
  107.4 8.4 %collective-permute-done.7 = f32[4,64,128]{2,1,0:T(8,128)S(1)} collective-permute-done((f32[4,64,128]{2,1,0:T(8,128)S(1)}, f32[4,64,128]{2,1,0:T(8,128)S(1)}, u32[]{:S(2)}, u32[]{:S(2)}) %collective-permute-start.7) | collective-permute-done | bytes 131104 | tf_op jit(solution)/shard_map/ppermute | solution.py:549
  115.9 2.3 collective-permute-start.10
  118.2 3.0 %collective-permute-start.9 = (f32[2,2,8,64,128]{4,3,2,1,0:T(8,128)S(1)}, f32[2,2,8,64,128]{4,3,2,1,0:T(8,128)}, u32[]{:S(2)}, u32[]{:S(2)}) collective-permute-start(f32[2,2,8,64,128]{4,3,2,1,0:T(8,128)S(1)} %bitcast.38), channel_id=1, source_target_pairs={{2,0},{3,1},{4,2},{5,3},{6,4},{7,5},{0,6},{1,7},{10,8},{11,9},{12,... | collective-permute-start | bytes 3145736 | tf_op jit(solution)/shard_map/ppermute | solution.py:557
  121.3 8.4 %shard_map.48.upper_ref = f32[8,16,64,128]{3,2,1,0:T(8,128)} custom-call(s32[51]{0:T(128)} %pad_add_fusion.1.tab, f32[8,16,2,64,128]{4,3,2,1,0:T(8,128)} %bitcast.31, f32[16,8,64,128]{3,2,1,0:T(8,128)} %bitcast.6.first_ref.other_ref, f32[16,8,64,128]{3,2,1,0:T(8,128)} %bitcast.6.first_ref.other_ref), custom_call_target="tpu_custom_call" | custom-call | flops 1024 | bytes 1024 | tf_op jit(solution)/shard_map/pallas_call | solution.py:179
  129.7 14.9 %collective-permute-done.10.refs_2_.refs_12_ = f32[2,2,8,64,128]{4,3,2,1,0:T(8,128)} collective-permute-done((f32[2,2,8,64,128]{4,3,2,1,0:T(8,128)S(1)}, f32[2,2,8,64,128]{4,3,2,1,0:T(8,128)}, u32[]{:S(2)}, u32[]{:S(2)}) %collective-permute-start.10) | collective-permute-done | bytes 1048608 | tf_op jit(solution)/shard_map/ppermute | solution.py:558
  144.5 1.1 slice.10
  145.6 2.5 collective-permute-start.11
  148.1 1.1 slice.11
  149.3 9.1 %collective-permute-done.11.refs_3_.refs_13_ = f32[1,2,8,64,128]{4,3,2,1,0:T(8,128)S(1)} collective-permute-done((f32[1,2,8,64,128]{4,3,2,1,0:T(8,128)S(1)}, f32[1,2,8,64,128]{4,3,2,1,0:T(8,128)S(1)}, u32[]{:S(2)}, u32[]{:S(2)}) %collective-permute-start.11) | collective-permute-done | bytes 524320 | tf_op jit(solution)/shard_map/ppermute | solution.py:562
  158.4 4.2 %collective-permute-done.12.refs_4_.refs_14_ = f32[1,2,8,64,128]{4,3,2,1,0:T(8,128)} collective-permute-done((f32[1,2,8,64,128]{4,3,2,1,0:T(8,128)S(1)}, f32[1,2,8,64,128]{4,3,2,1,0:T(8,128)}, u32[]{:S(2)}, u32[]{:S(2)}) %collective-permute-start.12) | collective-permute-done | bytes 524320 | tf_op jit(solution)/shard_map/ppermute | solution.py:563
  162.5 9.3 %all-to-all-start.1 = ((f32[128,64,128]{2,1,0:T(8,128)}), f32[128,64,128]{2,1,0:T(8,128)}, u32[]{:S(2)}, u32[]{:S(2)}) async-start(f32[128,64,128]{2,1,0:T(8,128)} %bitcast.35), calls=%async_computation.1 | async-start | bytes 8388608 | tf_op jit(solution)/shard_map/all_to_all | solution.py:569
  171.9 1.2 collective-permute-start.13
  174.7 1.2 collective-permute-done.13.refs_5_.refs_15_
  175.9 1.0 copy-done.1
  177.6 2.6 collective-permute-done.17.refs_9_.refs_19_
  180.2 59.9 %shard_map.50 = (bf16[1024,1024]{1,0:T(8,128)(2,1)}, bf16[1024,1024]{1,0:T(8,128)(2,1)}, f32[8,128,128]{2,1,0:T(8,128)}) custom-call(s32[4]{0:T(128)} %pad_add_fusion.3.at, f32[2,2,8,64,128]{4,3,2,1,0:T(8,128)} %bitcast.40, f32[2,2,8,64,128]{4,3,2,1,0:T(8,128)} %collective-permute-done.9.refs_1_.refs_11_, ...), custom_call_target="tpu_custom_call" | custom-call | flops 1024 | bytes 1024 | tf_op jit(solution)/shard_map/pallas_call | solution.py:369
  240.2 23.3 %shard_map.51 = f32[8,16,128,128]{3,2,1,0:T(8,128)} custom-call(s32[51]{0:T(128)} %pad_add_fusion.1.tab, f32[8,16,64,128]{3,2,1,0:T(8,128)} %shard_map.48.upper_ref, f32[8,16,2,64,128]{4,3,2,1,0:T(8,128)} %bitcast.32, f32[16,8,64,128]{3,2,1,0:T(8,128)} %bitcast.17.second_ref, f32[16,16,64,128]{3,2,1,0:T(8,128)} %bitcast.42, ...), custom_call_target="tpu_custom_call" | custom-call | flops 1024 | bytes 1024 | tf_op jit(solution)/shard_map/pallas_call | solution.py:458
  (54 shorter events, 8.8 us)
Async XLA Ops:
  13.4 66.4 %all-to-all-start = ((f32[128,64,128]{2,1,0:T(8,128)}), f32[128,64,128]{2,1,0:T(8,128)}, u32[]{:S(2)}, u32[]{:S(2)}) async-start(f32[128,64,128]{2,1,0:T(8,128)} %bitcast.36), calls=%async_computation | async-start | bytes 8388608 | tf_op jit(solution)/shard_map/all_to_all | solution.py:534
  25.4 214.8 %all-gather.3.cloned.1.call-start = ((), (), s32[]{:S(2)}) async-start(), calls=%async_computation.2 | async-start | bytes 8912896 | tf_op jit(solution)/shard_map/all_gather | solution.py:555
  26.5 8.8 %copy-start.4 = (s32[2,64]{1,0:T(2,128)S(1)}, s32[2,64]{1,0:T(2,128)}, u32[]{:S(2)}) copy-start(s32[2,64]{1,0:T(2,128)} %param.7) | copy-start | bytes 1540
  26.5 53.3 %collective-permute-start = (f32[16,64,128]{2,1,0:T(8,128)S(1)}, f32[16,64,128]{2,1,0:T(8,128)S(1)}, u32[]{:S(2)}, u32[]{:S(2)}) collective-permute-start(f32[16,64,128]{2,1,0:T(8,128)S(1)} %slice_bitcast_fusion), channel_id=1, source_target_pairs={{0,64},{8,72},{16,80},{24,88},{32,96},{40,104},{48,112},{56,120},{... | collective-permute-start | bytes 1572872 | tf_op jit(solution)/shard_map/ppermute | solution.py:531
  79.8 0.8 copy-start.3
  83.8 14.4 %collective-permute-start.1 = (f32[64,128]{1,0:T(8,128)}, f32[64,128]{1,0:T(8,128)S(1)}, u32[]{:S(2)}, u32[]{:S(2)}) collective-permute-start(f32[64,128]{1,0:T(8,128)} %get-tuple-element.30), channel_id=1, source_target_pairs={{8,0},{16,8},{24,16},{0,24},{40,32},{48,40},{56,48},{32,56},{72,64... | collective-permute-start | bytes 98312 | tf_op jit(solution)/shard_map/ppermute | solution.py:547
  87.6 10.6 %collective-permute-start.2 = (f32[64,128]{1,0:T(8,128)}, f32[64,128]{1,0:T(8,128)S(1)}, u32[]{:S(2)}, u32[]{:S(2)}) collective-permute-start(f32[64,128]{1,0:T(8,128)} %get-tuple-element.30), channel_id=1, source_target_pairs={{16,0},{24,8},{0,16},{8,24},{48,32},{56,40},{32,48},{40,56},{80,64... | collective-permute-start | bytes 98312 | tf_op jit(solution)/shard_map/ppermute | solution.py:547
  88.2 10.0 %collective-permute-start.3 = (f32[64,128]{1,0:T(8,128)}, f32[64,128]{1,0:T(8,128)S(1)}, u32[]{:S(2)}, u32[]{:S(2)}) collective-permute-start(f32[64,128]{1,0:T(8,128)} %get-tuple-element.30), channel_id=1, source_target_pairs={{24,0},{0,8},{8,16},{16,24},{56,32},{32,40},{40,48},{48,56},{88,64... | collective-permute-start | bytes 98312 | tf_op jit(solution)/shard_map/ppermute | solution.py:547
  89.3 26.5 %collective-permute-start.5 = (f32[8,64,128]{2,1,0:T(8,128)}, f32[8,64,128]{2,1,0:T(8,128)S(1)}, u32[]{:S(2)}, u32[]{:S(2)}) collective-permute-start(f32[8,64,128]{2,1,0:T(8,128)} %get-tuple-element.31), channel_id=1, source_target_pairs={{0,0},{1,9},{2,18},{3,27},{4,36},{5,45},{6,54},{7,63},{8,1},{9,8},... | collective-permute-start | bytes 786440 | tf_op jit(solution)/shard_map/ppermute | solution.py:544
  93.0 22.8 %collective-permute-start.8 = (f32[8,64,128]{2,1,0:T(8,128)}, f32[8,64,128]{2,1,0:T(8,128)S(1)}, u32[]{:S(2)}, u32[]{:S(2)}) collective-permute-start(f32[8,64,128]{2,1,0:T(8,128)} %get-tuple-element.32), channel_id=1, source_target_pairs={{0,64},{1,73},{2,82},{3,91},{4,100},{5,109},{6,118},{7,127},{8,65}... | collective-permute-start | bytes 786440 | tf_op jit(solution)/shard_map/ppermute | solution.py:545
  99.0 7.8 %collective-permute-start.4 = (f32[4,64,128]{2,1,0:T(8,128)S(1)}, f32[4,64,128]{2,1,0:T(8,128)S(1)}, u32[]{:S(2)}, u32[]{:S(2)}) collective-permute-start(f32[4,64,128]{2,1,0:T(8,128)S(1)} %pad_maximum_fusion.1), channel_id=1, source_target_pairs={{32,0},{40,8},{48,16},{56,24},{64,32},{72,40},{80,48},{88,56},{96,... | collective-permute-start | bytes 393224 | tf_op jit(solution)/shard_map/ppermute | solution.py:549
  101.7 5.7 %collective-permute-start.6 = (f32[4,64,128]{2,1,0:T(8,128)S(1)}, f32[4,64,128]{2,1,0:T(8,128)S(1)}, u32[]{:S(2)}, u32[]{:S(2)}) collective-permute-start(f32[4,64,128]{2,1,0:T(8,128)S(1)} %pad_maximum_fusion.1), channel_id=1, source_target_pairs={{64,0},{72,8},{80,16},{88,24},{96,32},{104,40},{112,48},{120,56},{... | collective-permute-start | bytes 393224 | tf_op jit(solution)/shard_map/ppermute | solution.py:549
  104.8 11.0 %collective-permute-start.7 = (f32[4,64,128]{2,1,0:T(8,128)S(1)}, f32[4,64,128]{2,1,0:T(8,128)S(1)}, u32[]{:S(2)}, u32[]{:S(2)}) collective-permute-start(f32[4,64,128]{2,1,0:T(8,128)S(1)} %pad_maximum_fusion.1), channel_id=1, source_target_pairs={{96,0},{104,8},{112,16},{120,24},{0,32},{8,40},{16,48},{24,56},{32... | collective-permute-start | bytes 393224 | tf_op jit(solution)/shard_map/ppermute | solution.py:549
  115.9 55.9 %copy-start = (f32[4,8,64,128]{3,2,1,0:T(8,128)}, f32[4,8,64,128]{3,2,1,0:T(8,128)S(1)}, u32[]{:S(2)}) copy-start(f32[4,8,64,128]{3,2,1,0:T(8,128)S(1)} %pad_maximum_fusion) | copy-start | bytes 3145732
  115.9 28.6 %collective-permute-start.10 = (f32[2,2,8,64,128]{4,3,2,1,0:T(8,128)S(1)}, f32[2,2,8,64,128]{4,3,2,1,0:T(8,128)}, u32[]{:S(2)}, u32[]{:S(2)}) collective-permute-start(f32[2,2,8,64,128]{4,3,2,1,0:T(8,128)S(1)} %bitcast.37), channel_id=1, source_target_pairs={{6,0},{7,1},{0,2},{1,3},{2,4},{3,5},{4,6},{5,7},{14,8},{15,9},{8,1... | collective-permute-start | bytes 3145736 | tf_op jit(solution)/shard_map/ppermute | solution.py:558
  118.2 26.3 %collective-permute-start.9 = (f32[2,2,8,64,128]{4,3,2,1,0:T(8,128)S(1)}, f32[2,2,8,64,128]{4,3,2,1,0:T(8,128)}, u32[]{:S(2)}, u32[]{:S(2)}) collective-permute-start(f32[2,2,8,64,128]{4,3,2,1,0:T(8,128)S(1)} %bitcast.38), channel_id=1, source_target_pairs={{2,0},{3,1},{4,2},{5,3},{6,4},{7,5},{0,6},{1,7},{10,8},{11,9},{12,... | collective-permute-start | bytes 3145736 | tf_op jit(solution)/shard_map/ppermute | solution.py:557
  145.6 12.8 %collective-permute-start.11 = (f32[1,2,8,64,128]{4,3,2,1,0:T(8,128)S(1)}, f32[1,2,8,64,128]{4,3,2,1,0:T(8,128)S(1)}, u32[]{:S(2)}, u32[]{:S(2)}) collective-permute-start(f32[1,2,8,64,128]{4,3,2,1,0:T(8,128)S(1)} %slice.10), channel_id=1, source_target_pairs={{2,0},{3,1},{4,2},{5,3},{6,4},{7,5},{0,6},{1,7},{10,8},{11,9},{12,... | collective-permute-start | bytes 1572872 | tf_op jit(solution)/shard_map/ppermute | solution.py:562
  149.2 13.3 %collective-permute-start.12 = (f32[1,2,8,64,128]{4,3,2,1,0:T(8,128)S(1)}, f32[1,2,8,64,128]{4,3,2,1,0:T(8,128)}, u32[]{:S(2)}, u32[]{:S(2)}) collective-permute-start(f32[1,2,8,64,128]{4,3,2,1,0:T(8,128)S(1)} %slice.11), channel_id=1, source_target_pairs={{6,0},{7,1},{0,2},{1,3},{2,4},{3,5},{4,6},{5,7},{14,8},{15,9},{8,1... | collective-permute-start | bytes 1572872 | tf_op jit(solution)/shard_map/ppermute | solution.py:563
  158.4 15.2 %copy-start.2 = (f32[1,2,8,64,128]{4,3,2,1,0:T(8,128)}, f32[1,2,8,64,128]{4,3,2,1,0:T(8,128)S(1)}, u32[]{:S(2)}) copy-start(f32[1,2,8,64,128]{4,3,2,1,0:T(8,128)S(1)} %collective-permute-done.11.refs_3_.refs_13_) | copy-start | bytes 1572868
  162.5 77.6 %all-to-all-start.1 = ((f32[128,64,128]{2,1,0:T(8,128)}), f32[128,64,128]{2,1,0:T(8,128)}, u32[]{:S(2)}, u32[]{:S(2)}) async-start(f32[128,64,128]{2,1,0:T(8,128)} %bitcast.35), calls=%async_computation.1 | async-start | bytes 8388608 | tf_op jit(solution)/shard_map/all_to_all | solution.py:569
  171.9 4.1 %collective-permute-start.13 = (f32[2,2,8,64,128]{4,3,2,1,0:T(8,128)S(1)}, f32[2,2,8,64,128]{4,3,2,1,0:T(8,128)S(1)}, u32[]{:S(2)}, u32[]{:S(2)}) collective-permute-start(f32[2,2,8,64,128]{4,3,2,1,0:T(8,128)S(1)} %bitcast.39), channel_id=1, source_target_pairs={{0,1},{1,0},{2,3},{3,2},{4,5},{5,4},{6,7},{7,6},{8,9},{9,8},{10,11... | collective-permute-start | bytes 3145736 | tf_op jit(solution)/shard_map/ppermute | solution.py:567
  173.1 7.1 %collective-permute-start.14 = (f32[2,2,8,64,128]{4,3,2,1,0:T(8,128)}, f32[2,2,8,64,128]{4,3,2,1,0:T(8,128)}, u32[]{:S(2)}, u32[]{:S(2)}) collective-permute-start(f32[2,2,8,64,128]{4,3,2,1,0:T(8,128)} %collective-permute-done.9.refs_1_.refs_11_), channel_id=1, source_target_pairs={{0,1},{1,0},{2,3},{3,2},{4,5},{5,4},{6,7},{7,6},{8,9},{9,8},{10,11... | collective-permute-start | bytes 3145736 | tf_op jit(solution)/shard_map/ppermute | solution.py:567
  173.2 7.0 %collective-permute-start.15 = (f32[2,2,8,64,128]{4,3,2,1,0:T(8,128)}, f32[2,2,8,64,128]{4,3,2,1,0:T(8,128)}, u32[]{:S(2)}, u32[]{:S(2)}) collective-permute-start(f32[2,2,8,64,128]{4,3,2,1,0:T(8,128)} %collective-permute-done.10.refs_2_.refs_12_), channel_id=1, source_target_pairs={{0,1},{1,0},{2,3},{3,2},{4,5},{5,4},{6,7},{7,6},{8,9},{9,8},{10,11... | collective-permute-start | bytes 3145736 | tf_op jit(solution)/shard_map/ppermute | solution.py:567
  173.6 4.0 %collective-permute-start.16 = (f32[1,2,8,64,128]{4,3,2,1,0:T(8,128)S(1)}, f32[1,2,8,64,128]{4,3,2,1,0:T(8,128)}, u32[]{:S(2)}, u32[]{:S(2)}) collective-permute-start(f32[1,2,8,64,128]{4,3,2,1,0:T(8,128)S(1)} %collective-permute-done.11.refs_3_.refs_13_), channel_id=1, source_target_pairs={{0,1},{1,0},{2,3},{3,2},{4,5},{5,4},{6,7},{7,6},{8,9},{9,8},{10,11... | collective-permute-start | bytes 1572872 | tf_op jit(solution)/shard_map/ppermute | solution.py:567
  173.7 6.5 %collective-permute-start.17 = (f32[1,2,8,64,128]{4,3,2,1,0:T(8,128)}, f32[1,2,8,64,128]{4,3,2,1,0:T(8,128)}, u32[]{:S(2)}, u32[]{:S(2)}) collective-permute-start(f32[1,2,8,64,128]{4,3,2,1,0:T(8,128)} %collective-permute-done.12.refs_4_.refs_14_), channel_id=1, source_target_pairs={{0,1},{1,0},{2,3},{3,2},{4,5},{5,4},{6,7},{7,6},{8,9},{9,8},{10,11... | collective-permute-start | bytes 1572872 | tf_op jit(solution)/shard_map/ppermute | solution.py:567
  175.9 1.0 copy-start.1
Sparse Core Ops, SparseCore 0:
  116.1 115.5 all-gather.2
